TPU v7x, 128 devices: a whole 4x4x4 slice. The times are simulated.
128 devices in a mesh: dp: 16 (over z, y), opt: 8 (over x, core).
Axes of the slice: x: 4, y: 4, z: 4, core: 2. Of those that a mesh axis runs over, the one named last changes fastest.
Arguments:
- grad_partial: bfloat16 [16, 96, 512, 512], P('dp', None, 'opt'), may hold values from -9 to 9
- master: float32 [96, 512, 512], P('dp', 'opt'), may hold values from -6 to 6
- second_moment: float32 [96, 512, 512], P('dp', 'opt'), may hold values from 0.01 to 1000
- owner_table: int32 [96, 1], replicated, may hold values from 0 to 7; in each aligned block of 6 rows (0 to 5, 6 to 11, ...) at most 2 rows name the same one
- factor_left: float32 [16, 8, 2, 512, 512], P('dp', 'opt'), may hold values from -0.2 to 2, as said below
- factor_right: float32 [16, 8, 2, 512, 512], P('dp', 'opt'), may hold values from -0.2 to 2, as said below
- root_left: bfloat16 [16, 8, 2, 512, 512], P('dp', 'opt'), may hold values from -0.15 to 1.5, as said below
- root_right: bfloat16 [16, 8, 2, 512, 512], P('dp', 'opt'), may hold values from -0.15 to 1.5, as said below
Outputs:
- master_new: float32 [96, 512, 512], P('dp', 'opt')
- moment_new: float32 [96, 512, 512], P('dp', 'opt')
- weights: bfloat16 [96, 512, 512], P(None, 'opt')
- left_new: float32 [16, 8, 2, 512, 512], P('dp', 'opt')
- right_new: float32 [16, 8, 2, 512, 512], P('dp', 'opt')
Inputs may be any that keep to these rules, and one draw needn't show every extreme that they name: `owner_table`: among the 6 blocks b = i * 6 to i * 6 + 5 of each i, no owner appears more than 2 times, and in every draw some owner appears exactly 2 times. `factor_left`: symmetric in the last two dimensions. `factor_right`: symmetric in the last two dimensions. `root_left`: symmetric in the last two dimensions. `root_right`: symmetric in the last two dimensions.
All inputs are finite; a program needn't handle non-finite values.
Results may differ from a plain program's by a relative error of at most 0.0015.
Values may be sent and summed in bfloat16 or wider, within the bound.
No kernel may reach another device: no remote copies, remote signals or barrier semaphores. Data moves between devices by JAX's collectives and lax.ppermute only.
A program may use at most 128 MiB of HBM per device.

v0:
```python
import jax
import jax.numpy as jnp
from jax import lax
from jax.sharding import PartitionSpec as P

BETA_FACTOR = 0.75
BETA_MOMENT = 0.95
LEARN_RATE = 0.1
EPS_ADAM = 1e-08
EPS_GRAFT = 1e-06


def slot_select(owners, owner_count, slot_count):
    block_count = owners.shape[0]
    position = jnp.arange(block_count)
    same_owner = owners[:, None] == owners[None, :]
    earlier = position[None, :] < position[:, None]
    slot_rank = jnp.sum((same_owner & earlier).astype(jnp.int32), axis=1)
    owner_hit = owners[None, None, :] == jnp.arange(owner_count)[:, None, None]
    rank_hit = slot_rank[None, None, :] == jnp.arange(slot_count)[None, :, None]
    return (owner_hit & rank_hit).astype(jnp.float32)


def shards(
    grad_partial,
    master,
    second_moment,
    owner_table,
    factor_left,
    factor_right,
    root_left,
    root_right,
):
    opt_count = lax.axis_size("opt")
    slot_count = factor_left.shape[2]
    row_blocks = master.shape[0]
    slab_rows = master.shape[1]
    block_width = master.shape[2]
    owner_list = owner_table[:, 0]
    own_owners = lax.dynamic_slice_in_dim(
        owner_list, lax.axis_index("dp") * row_blocks, row_blocks, 0
    )
    selector = slot_select(own_owners, opt_count, slot_count)
    grad_slab = lax.psum_scatter(
        grad_partial[0].astype(jnp.float32), "dp", scatter_dimension=0, tiled=True
    )
    outgoing = jnp.einsum("osk,krc->sorc", selector, grad_slab, precision=lax.Precision.HIGHEST)
    incoming = lax.all_to_all(outgoing, "opt", split_axis=1, concat_axis=1, tiled=True)
    owned_grad = incoming.reshape(slot_count, block_width, block_width)
    owned_count = jnp.sum((own_owners == lax.axis_index("opt")).astype(jnp.int32))
    occupied = (jnp.arange(slot_count) < owned_count)[:, None, None]
    gram_left = (
        jnp.einsum("sab,scb->sac", owned_grad, owned_grad, precision=lax.Precision.HIGHEST)
        / block_width
    )
    gram_right = (
        jnp.einsum("sba,sbc->sac", owned_grad, owned_grad, precision=lax.Precision.HIGHEST)
        / block_width
    )
    left_states = factor_left[0, 0]
    right_states = factor_right[0, 0]
    left_new = jnp.where(
        occupied, BETA_FACTOR * left_states + (1.0 - BETA_FACTOR) * gram_left, left_states
    )
    right_new = jnp.where(
        occupied, BETA_FACTOR * right_states + (1.0 - BETA_FACTOR) * gram_right, right_states
    )
    half_product = jnp.einsum(
        "sab,sbc->sac",
        root_left[0, 0],
        owned_grad.astype(jnp.bfloat16),
        preferred_element_type=jnp.float32,
    ).astype(jnp.bfloat16)
    direction = jnp.einsum(
        "sab,sbc->sac", half_product, root_right[0, 0], preferred_element_type=jnp.float32
    )
    direction_rows = direction.reshape(slot_count, opt_count, slab_rows, block_width)
    returned = lax.all_to_all(direction_rows, "opt", split_axis=1, concat_axis=1, tiled=True)
    direction_slab = jnp.einsum(
        "osk,sorc->krc", selector, returned, precision=lax.Precision.HIGHEST
    )
    moment_new = BETA_MOMENT * second_moment + (1.0 - BETA_MOMENT) * grad_slab * grad_slab
    adam_step = grad_slab / (jnp.sqrt(moment_new) + EPS_ADAM)
    adam_square = jnp.sum(adam_step * adam_step, axis=(1, 2))
    direction_square = jnp.sum(direction_slab * direction_slab, axis=(1, 2))
    adam_square, direction_square = lax.psum((adam_square, direction_square), "opt")
    graft_scale = jnp.sqrt(adam_square) / (jnp.sqrt(direction_square) + EPS_GRAFT)
    master_new = master - LEARN_RATE * graft_scale[:, None, None] * direction_slab
    weights = lax.all_gather(master_new.astype(jnp.bfloat16), "dp", axis=0, tiled=True)
    return (master_new, moment_new, weights, left_new[None, None], right_new[None, None])


def solution(mesh):
    placed = (
        P("dp", None, "opt", None),
        P("dp", "opt", None),
        P("dp", "opt", None),
        P(),
        P("dp", "opt", None, None, None),
        P("dp", "opt", None, None, None),
        P("dp", "opt", None, None, None),
        P("dp", "opt", None, None, None),
    )
    return jax.shard_map(
        shards,
        mesh=mesh,
        in_specs=placed,
        out_specs=(
            P("dp", "opt", None),
            P("dp", "opt", None),
            P(None, "opt", None),
            P("dp", "opt", None, None, None),
            P("dp", "opt", None, None, None),
        ),
        check_vma=False,
    )
```

profile of v0, /device:TPU:0, one launch (start us, length us, event | category | flops | bytes accessed | tf_op | source)
XLA Modules:
  0.0 284.0 jit_solution(13872888802348377428)
XLA Ops:
  7.2 0.0 copy-start
  7.2 0.0 reduce-scatter.2.cloned.1.call-start
  7.2 9.3 %bitcast_convert_fusion = f32[96,64,512]{2,1,0:T(8,128)} fusion(bf16[1,96,64,512]{3,2,1,0:T(8,128)(2,1)} %param.8), kind=kLoop, calls=%fused_computation | loop fusion | flops 3145728 | bytes 18874368 | tf_op jit(solution)/shard_map/convert_element_type | solution.py:45
  16.5 0.0 copy-start.3
  16.5 0.0 reduce-scatter.2.cloned.1.call-update
  16.6 0.6 copy-done.3
  17.2 0.7 fusion.23
  17.9 0.2 convert_reduce_fusion
  18.1 0.1 iota_compare_fusion.1
  18.2 95.9 %reduce-scatter.2.cloned.1.call-done = f32[6,64,512]{2,1,0:T(8,128)} async-done(((f32[96,64,512]{2,1,0:T(8,128)}), f32[6,64,512]{2,1,0:T(8,128)}) %reduce-scatter.2.cloned.1.call-update) | async-done | bytes 786448 | tf_op jit(solution)/shard_map/reduce_scatter | solution.py:44
  114.0 2.6 convolution_bitcast_fusion
  116.6 1.2 copy.42
  117.9 31.6 %all_to_all.10 = f32[2,8,64,512]{3,2,0,1:T(8,128)S(1)} all-to-all(f32[2,8,64,512]{3,2,0,1:T(8,128)S(1)} %copy.42), channel_id=1, replica_groups=mesh['dp'=16,'opt'=8] {'opt'}, dimensions={1} | all-to-all | bytes 4194304 | tf_op jit(solution)/shard_map/all_to_all | solution.py:48
  149.4 0.2 copy.43
  149.6 1.4 copy.44
  151.0 0.0 copy-done
  151.0 4.1 %fusion.6 = f32[2,512,512]{2,1,0:T(8,128)} fusion(bf16[1,1,2,512,512]{4,3,2,1,0:T(8,128)(2,1)S(1)} %copy-done, bf16[1,1,2,512,512]{4,3,2,1,0:T(8,128)(2,1)} %param.14, bf16[2,512,512]{1,2,0:T(8,128)(2,1)} %copy.44), kind=kOutput, calls=%fused_computation.13 | convolution fusion | flops 1074266112 | bytes 5242880 | tf_op jit(solution)/shard_map/sab,sbc->sac/dot_general | solution.py:74
  155.2 4.5 %copy.46 = f32[2,8,64,512]{3,0,2,1:T(2,128)} copy(f32[2,8,64,512]{3,2,1,0:T(8,128)} %bitcast.63) | data formatting | bytes 4194304 | tf_op jit(solution)/shard_map/reshape | solution.py:77
  159.7 4.3 %all-to-all-start.1 = ((f32[2,8,64,512]{3,0,2,1:T(2,128)}), f32[2,8,64,512]{3,0,2,1:T(2,128)}, u32[]{:S(2)}, u32[]{:S(2)}) async-start(f32[2,8,64,512]{3,0,2,1:T(2,128)} %copy.46), calls=%async_computation.2 | async-start | bytes 4194304 | tf_op jit(solution)/shard_map/all_to_all | solution.py:78
  164.0 0.0 all-gather.2.cloned.1.call-start
  164.1 2.7 multiply_reduce_fusion.1
  166.7 24.5 %all-to-all-done.1 = f32[2,8,64,512]{3,0,2,1:T(2,128)} async-done(((f32[2,8,64,512]{3,0,2,1:T(2,128)}), f32[2,8,64,512]{3,0,2,1:T(2,128)}, u32[]{:S(2)}, u32[]{:S(2)}) %all-to-all-start.1) | async-done | bytes 2097184 | tf_op jit(solution)/shard_map/all_to_all | solution.py:78
  191.2 4.7 %multiply_reduce_fusion = (f32[6]{0:T(128)S(1)}, f32[6,64,512]{2,0,1:T(8,128)}) fusion(f32[2,8,64,512]{3,0,2,1:T(2,128)} %all-to-all-done.1, pred[2,6]{1,0:T(4,128)(4,1)S(1)} %iota_compare_fusion.2, pred[8,6]{0,1:T(8,128)(4,1)S(1)} %iota_compare_fusion.1), kind=kOutput, calls=%fused_computation.21 | convolution fusion | flops 38142040 | bytes 2883668 | tf_op jit(solution)/shard_map/osk,sorc->krc/dot_general | solution.py:79
  195.9 13.0 %all-reduce = (f32[6]{0:T(128)S(1)}, f32[6]{0:T(128)S(1)}) all-reduce(f32[6]{0:T(128)S(1)} %get-tuple-element.33, f32[6]{0:T(128)S(1)} %get-tuple-element.31), channel_id=1, replica_groups=mesh['dp'=16,'opt'=8] {'opt'}, use_global_device_ids=true, to_apply=%region_5.6 | all-reduce | flops 12 | bytes 96 | tf_op jit(solution)/shard_map/psum | solution.py:86
  208.9 3.0 %fusion.25 = (bf16[6,64,512]{2,0,1:T(8,128)(2,1)S(1)}, f32[6,64,512]{2,0,1:T(8,128)}) fusion(f32[6,64,512]{2,0,1:T(8,128)} %get-tuple-element.34, f32[6]{0:T(128)S(1)} %fusion.24, f32[6,64,512]{2,1,0:T(8,128)} %param.9), kind=kLoop, calls=%fused_computation.42 | loop fusion | flops 589824 | bytes 2752536 | tf_op jit(solution)/shard_map/convert_element_type | solution.py:89
  211.9 0.9 copy.49
  212.8 0.0 all-gather.2.cloned.1.call-update
  212.8 0.7 iota_compare_fusion.3
  213.5 0.0 copy-start.2
  213.5 6.1 %fusion.3 = f32[1,1,2,512,512]{4,3,2,1,0:T(8,128)} fusion(f32[1,1,2,512,512]{4,3,2,1,0:T(8,128)} %param.12, f32[2,512,512]{2,1,0:T(8,128)S(1)} %bitcast.61, pred[2]{0:T(512)(128)(4,1)S(1)} %iota_compare_fusion.3), kind=kOutput, calls=%fused_computation.8 | convolution fusion | flops 3223322624 | bytes 6291458 | tf_op jit(solution)/shard_map/sab,scb->sac/dot_general | solution.py:53
  219.6 0.0 copy-done.2
  219.6 0.0 copy-start.1
  219.6 5.2 %fusion.1 = f32[1,1,2,512,512]{4,3,2,1,0:T(8,128)} fusion(f32[1,1,2,512,512]{4,3,2,1,0:T(8,128)S(1)} %copy-done.2, f32[2,512,512]{2,1,0:T(8,128)S(1)} %bitcast.62, pred[2]{0:T(512)(128)(4,1)S(1)} %iota_compare_fusion.3), kind=kOutput, calls=%fused_computation.4 | convolution fusion | flops 3223322624 | bytes 6291458 | tf_op jit(solution)/shard_map/sba,sbc->sac/dot_general | solution.py:57
  224.9 0.0 copy-done.1
  224.9 1.3 copy.51
  226.2 44.7 %all-gather.2.cloned.1.call-done = bf16[96,64,512]{2,1,0:T(8,128)(2,1)} async-done(((bf16[6,64,512]{2,1,0:T(8,128)(2,1)}), bf16[96,64,512]{2,1,0:T(8,128)(2,1)}) %all-gather.2.cloned.1.call-update) | async-done | bytes 6291472 | tf_op jit(solution)/shard_map/all_gather | solution.py:89
  270.9 6.3 %copy.71 = bf16[96,64,512]{2,1,0:T(8,128)(2,1)} copy(bf16[96,64,512]{2,1,0:T(8,128)(2,1)} %all-gather.2.cloned.1.call-done) | data formatting | bytes 12582912
  (2 shorter events, 0.0 us)
Async XLA Ops:
  7.2 143.8 %copy-start = (bf16[1,1,2,512,512]{4,3,2,1,0:T(8,128)(2,1)S(1)}, bf16[1,1,2,512,512]{4,3,2,1,0:T(8,128)(2,1)}, u32[]{:S(2)}) copy-start(bf16[1,1,2,512,512]{4,3,2,1,0:T(8,128)(2,1)} %param.15) | copy-start | bytes 3145732
  7.2 106.9 %reduce-scatter.2.cloned.1.call-start = ((), (), s32[]{:S(2)}) async-start(), calls=%async_computation.3 | async-start | bytes 13369344 | tf_op jit(solution)/shard_map/reduce_scatter | solution.py:44
  16.5 0.7 copy-start.3
  159.7 31.5 %all-to-all-start.1 = ((f32[2,8,64,512]{3,0,2,1:T(2,128)}), f32[2,8,64,512]{3,0,2,1:T(2,128)}, u32[]{:S(2)}, u32[]{:S(2)}) async-start(f32[2,8,64,512]{3,0,2,1:T(2,128)} %copy.46), calls=%async_computation.2 | async-start | bytes 4194304 | tf_op jit(solution)/shard_map/all_to_all | solution.py:78
  164.0 106.9 %all-gather.2.cloned.1.call-start = ((), (), s32[]{:S(2)}) async-start(), calls=%async_computation.4 | async-start | bytes 6684672 | tf_op jit(solution)/shard_map/all_gather | solution.py:89
  213.5 6.2 %copy-start.2 = (f32[1,1,2,512,512]{4,3,2,1,0:T(8,128)S(1)}, f32[1,1,2,512,512]{4,3,2,1,0:T(8,128)}, u32[]{:S(2)}) copy-start(f32[1,1,2,512,512]{4,3,2,1,0:T(8,128)} %param.13) | copy-start | bytes 6291460
  219.6 5.2 %copy-start.1 = (f32[6,64,512]{2,0,1:T(8,128)S(1)}, f32[6,64,512]{2,0,1:T(8,128)}, u32[]{:S(2)}) copy-start(f32[6,64,512]{2,0,1:T(8,128)} %get-tuple-element.30) | copy-start | bytes 2359300
Sparse Core Ops, SparseCore 0:
  16.7 97.3 reduce-scatter.1
  212.9 57.9 all-gather.1
where the time goes:
time: 285 us; the launch traced here: 284 us
  waiting for transfers between devices  165 us (58%)
  blocking collectives  44.5 us (16%)
  matrix products  22.8 us (8%)
  other arithmetic  16.6 us (6%)
  local copies, waits for them, and re-layouts  16.5 us (6%)
  between operations  14.1 us (5%)
  starting transfers between devices  4.42 us (2%)
    reduce_scatter x1, waiting for transfers between devices, shards(): lax.psum_scatter(grad_partial[0].astype(jnp.float32), 'dp', scatter_dimen...  95.9 us
    all_gather x1, waiting for transfers between devices, shards(): lax.all_gather(master_new.astype(jnp.bfloat16), 'dp', axis=0, tiled=True)  44.7 us
    all_to_all x1, blocking collectives, shards(): lax.all_to_all(outgoing, 'opt', split_axis=1, concat_axis=1, tiled=True)  31.6 us
    all_to_all x1, waiting for transfers between devices, shards(): lax.all_to_all(direction_rows, 'opt', split_axis=1, concat_axis=1, tiled=...  24.5 us
    psum x1, blocking collectives, shards(): lax.psum((adam_square, direction_square), 'opt')  13 us
    convert_element_type x1, other arithmetic, shards(): grad_partial[0].astype(jnp.float32)  9.31 us
    unnamed x10, local copies, waits for them, and re-layouts  8.28 us
    dot_general x1, matrix products, shards(): jnp.einsum('sab,scb->sac', owned_grad, owned_grad, precision=lax.Precisio...  6.14 us
  transfers between devices with their start and end apart: 3, of which 3 were waited for; matrix products, arithmetic and copies ran while one was open for 6% of the time, Pallas kernels for 0%

commit v1 on v0

v1 whole, which is shorter than its diff:
```python
import functools

import jax
import jax.numpy as jnp
from jax import lax
from jax.experimental import pallas as pl
from jax.experimental.pallas import tpu as pltpu
from jax.sharding import PartitionSpec as P

BETA_FACTOR = 0.75
BETA_MOMENT = 0.95
LEARN_RATE = 0.1
EPS_ADAM = 1e-08
EPS_GRAFT = 1e-06
SIDE = 4
CHUNKS = ((0, 3), (3, 6))
VMEM = 60 * 2**20


def shift_perm(axis, step):
    pairs = []
    for z in range(SIDE):
        for y in range(SIDE):
            to_z = (z + step) % SIDE if axis == "z" else z
            to_y = (y + step) % SIDE if axis == "y" else y
            pairs.append((z * SIDE + y, to_z * SIDE + to_y))
    return pairs


def send(value, axis, step):
    return lax.ppermute(value, "dp", shift_perm(axis, step))


def after(value, *earlier):
    return lax.optimization_barrier((value,) + earlier)[0]


ORDER = (("y", 1), ("z", 1), ("y", 3), ("z", 3), ("y", 2), ("z", 2))
OTHER = {"y": "z", "z": "y"}


def exchange(make):
    got = {}
    for axis, step in ORDER:
        value = make(axis, step)
        got[axis, step] = send(after(value, got["z", 1]) if (axis, step) == ORDER[-1] else value, axis, step)
    return got


def together(got):
    return dict(zip(got, lax.optimization_barrier(tuple(got.values()))))


def sum_replicas(parts, place, needed):
    blocks, half_rows, width = parts.shape[2], parts.shape[3] // 2, parts.shape[4]
    top = {"y": 0, "z": half_rows}

    def raw(axis, step):
        at = (place[axis] + step) % SIDE
        start = (0, at, 0, top[axis], 0) if axis == "y" else (at, 0, 0, top[axis], 0)
        size = (SIDE, 1) if axis == "y" else (1, SIDE)
        got = lax.dynamic_slice(parts, start, size + (blocks, half_rows, width))
        return got.reshape((SIDE, blocks, half_rows, width))

    near = together(exchange(raw))

    def total(chunk, axis, step):
        first, last = chunk
        at = (place[axis] + step) % SIDE
        axis = OTHER[axis]
        start = (at, place["y"]) if axis == "y" else (place["z"], at)
        size = (last - first, half_rows, width)
        own = lax.dynamic_slice(parts, start + (first, top[axis], 0), (1, 1) + size)[0, 0]
        picked = [lax.dynamic_slice(near[axis, hop], (at, first, 0, 0), (1,) + size)[0] for hop in (1, 3, 2)]
        own, one, three, two = [part.astype(jnp.float32) for part in [own] + picked]
        return (own + one) + (three + two)

    parcels = []
    for number, chunk in enumerate(CHUNKS):
        make = functools.partial(total, chunk)
        if parcels:
            behind = parcels[-1][2]
            far = exchange(lambda axis, step: after(make(axis, step), behind))
        else:
            far = exchange(make)
        far = together(far)
        halves = []
        for axis in ("y", "z"):
            one, three, two = [far[OTHER[axis], step] for step in (1, 3, 2)]
            halves.append((total(chunk, OTHER[axis], 0) + one) + (after(three, *needed[number]) + two))
        grad = jnp.concatenate(halves, axis=1)
        rounded = lax.reduce_precision(grad, 8, 7)
        parcels.append((grad, rounded, rounded.astype(jnp.bfloat16)))
    return parcels


def place_kernel(step, first, place_ref, upper_ref, lower_ref, *refs):
    out, sems = refs[-2:]
    z, y = place_ref[0], place_ref[1]
    still_z, still_y = lax.rem(z + SIDE - step, SIDE), lax.rem(y + SIDE - step, SIDE)
    blocks, rows = pl.ds(first, upper_ref.shape[1]), upper_ref.shape[2]
    copies = []
    for hop in range(SIDE):
        upper = out.at[still_z, lax.rem(y + SIDE - hop, SIDE), blocks, pl.ds(0, rows)]
        lower = out.at[lax.rem(z + SIDE - hop, SIDE), still_y, blocks, pl.ds(rows, rows)]
        copies.append(pltpu.make_async_copy(upper_ref.at[hop], upper, sems.at[hop]))
        copies.append(pltpu.make_async_copy(lower_ref.at[hop], lower, sems.at[SIDE + hop]))
    for copy in copies:
        copy.start()
    for copy in copies:
        copy.wait()


def put(out, shape, place, step, upper, lower, first):
    spot = jnp.stack([place["z"], place["y"]]).astype(jnp.int32)
    before = [] if out is None else [out]
    piece = pl.BlockSpec(upper.shape, lambda t: (0, 0, 0, 0))
    return pl.pallas_call(
        functools.partial(place_kernel, step, first),
        grid=(1,),
        out_shape=jax.ShapeDtypeStruct(shape, jnp.bfloat16),
        in_specs=[pl.BlockSpec(memory_space=pltpu.SMEM)]
        + [piece, piece]
        + [pl.BlockSpec(memory_space=pl.ANY)] * len(before),
        out_specs=pl.BlockSpec(memory_space=pl.ANY),
        scratch_shapes=[pltpu.SemaphoreType.DMA((2 * SIDE,))],
        input_output_aliases={3: 0} if before else {},
        compiler_params=pltpu.CompilerParams(vmem_limit_bytes=8 * 2**20),
        cost_estimate=pl.CostEstimate(flops=0, bytes_accessed=8 * upper.size, transcendentals=0),
        name="place_weights",
    )(spot, upper, lower, *before)


def direction_kernel(owner_ref, rank_ref, left_ref, grad_ref, right_ref, out_ref, square_ref):
    width = right_ref.shape[-1]
    grad = grad_ref[...].reshape(width, width)
    half = jnp.dot(left_ref[0, 0], grad, preferred_element_type=jnp.float32).astype(jnp.bfloat16)
    rows = jnp.dot(half, right_ref[0, 0], preferred_element_type=jnp.float32)
    out_ref[0] = rows
    square_ref[...] = jnp.full(square_ref.shape, jnp.sum(rows * rows), jnp.float32)


def directions(owner, rank, left_rows, grad_whole, right_roots):
    opt_count, blocks, slab_rows, width = grad_whole.shape
    grid_spec = pltpu.PrefetchScalarGridSpec(
        num_scalar_prefetch=2,
        grid=(blocks,),
        in_specs=[
            pl.BlockSpec((1, 1, slab_rows, width), lambda k, owner, rank: (rank[k], owner[k], 0, 0)),
            pl.BlockSpec((opt_count, 1, slab_rows, width), lambda k, owner, rank: (0, k, 0, 0)),
            pl.BlockSpec((1, 1, width, width), lambda k, owner, rank: (owner[k], rank[k], 0, 0)),
        ],
        out_specs=[
            pl.BlockSpec((1, slab_rows, width), lambda k, owner, rank: (k, 0, 0)),
            pl.BlockSpec((1, 8, 128), lambda k, owner, rank: (k, 0, 0)),
        ],
    )
    flops = blocks * 4 * slab_rows * width * width
    return pl.pallas_call(
        direction_kernel,
        grid_spec=grid_spec,
        out_shape=[
            jax.ShapeDtypeStruct((blocks, slab_rows, width), jnp.float32),
            jax.ShapeDtypeStruct((blocks, 8, 128), jnp.float32),
        ],
        compiler_params=pltpu.CompilerParams(vmem_limit_bytes=VMEM),
        cost_estimate=pl.CostEstimate(
            flops=flops, bytes_accessed=blocks * width * width * 4, transcendentals=0
        ),
        name="directions",
    )(owner, rank, left_rows, grad_whole, right_roots)


def gram_kernel(block_ref, used_ref, *refs):
    highs = refs[: len(CHUNKS)]
    low_ref, left_ref, right_ref, left_out, right_out, high_ref = refs[len(CHUNKS) :]
    slot = pl.program_id(0)
    width = left_ref.shape[-1]
    for number, (first, last) in enumerate(CHUNKS):

        @pl.when((block_ref[slot] >= first) & (block_ref[slot] < last))
        def _():
            high_ref[...] = highs[number][...].reshape(width, width)

    @pl.when(used_ref[slot] == 1)
    def _():
        high = high_ref[...]
        low = low_ref[...].reshape(width, width)
        scale = (1.0 - BETA_FACTOR) / width

        def gram(dims):
            dot = functools.partial(
                lax.dot_general, dimension_numbers=(dims, ((), ())), preferred_element_type=jnp.float32
            )
            cross = dot(high, low)
            return dot(high, high) + (cross + cross.T)

        left_out[0, 0, 0] = BETA_FACTOR * left_ref[0, 0, 0] + scale * gram(((1,), (1,)))
        right_out[0, 0, 0] = BETA_FACTOR * right_ref[0, 0, 0] + scale * gram(((0,), (0,)))

    @pl.when(used_ref[slot] == 0)
    def _():
        left_out[...] = left_ref[...]
        right_out[...] = right_ref[...]


def factors(block_at, used, highs, low, factor_left, factor_right):
    slot_count, width = factor_left.shape[2], factor_left.shape[-1]
    opt_count, _, slab_rows, _ = low.shape

    def grad_spec(first, last):
        def at_block(s, at, used):
            return (0, jnp.clip(at[s] - first, 0, last - first - 1), 0, 0)

        return pl.BlockSpec((opt_count, 1, slab_rows, width), at_block)

    state_spec = pl.BlockSpec((1, 1, 1, width, width), lambda s, at, used: (0, 0, s, 0, 0))
    grid_spec = pltpu.PrefetchScalarGridSpec(
        num_scalar_prefetch=2,
        grid=(slot_count,),
        in_specs=[grad_spec(*chunk) for chunk in CHUNKS]
        + [grad_spec(0, CHUNKS[-1][1]), state_spec, state_spec],
        out_specs=[state_spec, state_spec],
        scratch_shapes=[pltpu.VMEM((width, width), jnp.bfloat16)],
    )
    return pl.pallas_call(
        gram_kernel,
        grid_spec=grid_spec,
        out_shape=[jax.ShapeDtypeStruct(factor_left.shape, jnp.float32)] * 2,
        compiler_params=pltpu.CompilerParams(vmem_limit_bytes=VMEM),
        cost_estimate=pl.CostEstimate(
            flops=slot_count * 12 * width**3,
            bytes_accessed=slot_count * 20 * width * width,
            transcendentals=0,
        ),
        name="factors",
    )(block_at, used, *highs, low, factor_left, factor_right)


def spread_weights(weights):
    half_rows = weights.shape[1] // 2
    own = {"y": weights[:, :half_rows], "z": weights[:, half_rows:]}
    near = exchange(lambda axis, step: own[axis])
    begun = near["y", 1]
    near = together(near)
    line = {axis: jnp.stack([own[axis]] + [near[axis, hop] for hop in (1, 2, 3)]) for axis in own}
    return begun, line, exchange(lambda axis, step: line[OTHER[axis]])


def put_all(out, shape, place, line, far, first):
    out = put(out, shape, place, 0, line["y"], line["z"], first)
    for step in (1, 3, 2):
        out = put(out, shape, place, step, far["z", step], far["y", step], first)
    return out


def shards(
    grad_partial,
    master,
    second_moment,
    owner_table,
    factor_left,
    factor_right,
    root_left,
    root_right,
):
    opt_count = lax.axis_size("opt")
    slot_count = factor_left.shape[2]
    row_blocks, slab_rows, width = master.shape
    dp_at, opt_at = lax.axis_index("dp"), lax.axis_index("opt")
    place = {"z": dp_at // SIDE, "y": dp_at % SIDE}

    owner = lax.dynamic_slice_in_dim(owner_table[:, 0], dp_at * row_blocks, row_blocks, 0)
    position = jnp.arange(row_blocks)
    same_owner = owner[:, None] == owner[None, :]
    earlier = position[None, :] < position[:, None]
    rank = jnp.sum((same_owner & earlier).astype(jnp.int32), axis=1)
    mine = (owner[None, :] == opt_at) & (rank[None, :] == jnp.arange(slot_count)[:, None])
    used = jnp.sum(mine.astype(jnp.int32), axis=1)
    block_at = jnp.sum(jnp.where(mine, position[None, :], 0), axis=1).astype(jnp.int32)

    right_roots = lax.all_gather(root_right[0, 0], "opt", axis=0)
    left_rows = lax.all_to_all(
        root_left[0, 0].reshape(slot_count, opt_count, slab_rows, width),
        "opt",
        split_axis=1,
        concat_axis=1,
        tiled=True,
    )

    parts = grad_partial[0].reshape(SIDE, SIDE, row_blocks, slab_rows, width)
    parcels = sum_replicas(parts, place, ((left_rows, right_roots), ()))

    lows, wholes, masters, moments, sent = [], [], [], [], []
    for number, (first, last) in enumerate(CHUNKS):
        grad, rounded, high = parcels[number]
        lows.append((grad - rounded).astype(jnp.bfloat16))
        if number > 0:
            high = after(high, wholes[-1])
        wholes.append(lax.all_gather(high, "opt", axis=0))
        moment = BETA_MOMENT * second_moment[first:last] + (1.0 - BETA_MOMENT) * grad * grad
        step = grad / (jnp.sqrt(moment) + EPS_ADAM)
        adam_square = jnp.sum(step * step, axis=(1, 2))
        whole = wholes[number] if number == 0 else after(wholes[number], sent[0][0])
        rows, row_square = directions(owner[first:last], rank[first:last], left_rows, whole, right_roots)
        squares = jnp.concatenate(
            [jnp.broadcast_to(adam_square[:, None, None], row_square.shape), row_square], axis=0
        )
        squares = jnp.broadcast_to(squares[None], (opt_count,) + squares.shape)
        squares = lax.all_to_all(squares, "opt", split_axis=0, concat_axis=0, tiled=True)
        if number > 0:
            squares = after(squares, *[sent[0][2][key] for key in ORDER[:4]])
        adam_total, row_total = jnp.split(jnp.sum(squares, axis=0)[:, 0, 0], 2)
        graft_scale = jnp.sqrt(adam_total) / (jnp.sqrt(row_total) + EPS_GRAFT)
        fresh = master[first:last] - LEARN_RATE * graft_scale[:, None, None] * rows
        sent.append(spread_weights(fresh.astype(jnp.bfloat16)))
        masters.append(fresh)
        moments.append(moment)

    low_whole = lax.all_gather(after(jnp.concatenate(lows), squares), "opt", axis=0)
    left_new, right_new = factors(block_at, used, wholes, low_whole, factor_left, factor_right)
    sent[0][1]["y"] = after(sent[0][1]["y"], sent[1][2]["y", 1])
    gathered = put_all(None, parts.shape, place, *sent[0][1:], 0)
    sent[1][1]["y"] = after(sent[1][1]["y"], left_new)
    gathered = put_all(gathered, parts.shape, place, *sent[1][1:], CHUNKS[1][0])
    return (
        jnp.concatenate(masters, axis=0),
        jnp.concatenate(moments, axis=0),
        gathered.reshape(-1, slab_rows, width),
        left_new,
        right_new,
    )


def solution(mesh):
    placed = (
        P("dp", None, "opt", None),
        P("dp", "opt", None),
        P("dp", "opt", None),
        P(),
        P("dp", "opt", None, None, None),
        P("dp", "opt", None, None, None),
        P("dp", "opt", None, None, None),
        P("dp", "opt", None, None, None),
    )
    return jax.shard_map(
        shards,
        mesh=mesh,
        in_specs=placed,
        out_specs=(
            P("dp", "opt", None),
            P("dp", "opt", None),
            P(None, "opt", None),
            P("dp", "opt", None, None, None),
            P("dp", "opt", None, None, None),
        ),
        check_vma=False,
    )
```

time: 285 us -> 229 us (0.80)
  waiting for transfers between devices: 165 us -> 66.6 us
  starting transfers between devices: 4.42 us -> 71.4 us
  blocking collectives: 44.5 us -> 11.9 us
  Pallas kernels: 0 us -> 27.8 us
  matrix products: 22.8 us -> 0 us
  other arithmetic: 16.6 us -> 23.4 us
  local copies, waits for them, and re-layouts: 16.5 us -> 11.1 us
    reduce_scatter x1 -> x0, waiting for transfers between devices: 95.9 us -> none  [shards(): lax.psum_scatter(grad_partial[0].astype(jnp.float32), 'dp', scatter_dimen...]
    ppermute x0 -> x42, starting transfers between devices: none -> 63.6 us  [send(): return lax.ppermute(value, 'dp', shift_perm(axis, step))]
    ppermute x0 -> x42, waiting for transfers between devices: none -> 55.9 us  [send(): return lax.ppermute(value, 'dp', shift_perm(axis, step))]
    all_gather x1 -> x4, waiting for transfers between devices: 44.7 us -> 4.99 us  [the longest x2 4.97 us: shards(): wholes.append(lax.all_gather(high, 'opt', axis=0))]
    pallas_call x0 -> x11, Pallas kernels: none -> 27.8 us  [the longest x8 13.1 us: put(): pl.pallas_call(functools.partial(place_kernel, step, first), grid=(1,), o...]
    dot_general x5 -> x0, matrix products: 22.8 us -> none  [the longest x1 6.14 us: shards(): jnp.einsum('sab,scb->sac', owned_grad, owned_grad, precision=lax.Precisio...]
    all_to_all x1, blocking collectives: 31.6 us -> 11.9 us  [shards(): lax.all_to_all(squares, 'opt', split_axis=0, concat_axis=0, tiled=True)]
    all_to_all x1 -> x2, waiting for transfers between devices: 24.5 us -> 4.98 us  [the longest x1 4.97 us: shards(): lax.all_to_all(squares, 'opt', split_axis=0, concat_axis=0, tiled=True)]
  transfers between devices with their start and end apart: 3 -> 48, of which waited for: 3 -> 18; matrix products, arithmetic and copies ran while one was open for 6% -> 13% of each run, Pallas kernels for 0% -> 11%
where the time goes in v1:
time: 229 us; the launch traced here: 226 us
  starting transfers between devices  71.4 us (31%)
  waiting for transfers between devices  66.6 us (29%)
  Pallas kernels  27.8 us (12%)
  other arithmetic  23.4 us (10%)
  between operations  14.3 us (6%)
  blocking collectives  11.9 us (5%)
  local copies, waits for them, and re-layouts  11.1 us (5%)
    ppermute x42, starting transfers between devices, send(): return lax.ppermute(value, 'dp', shift_perm(axis, step))  63.6 us
    ppermute x42, waiting for transfers between devices, send(): return lax.ppermute(value, 'dp', shift_perm(axis, step))  55.9 us
    pallas_call x8, Pallas kernels, put(): pl.pallas_call(functools.partial(place_kernel, step, first), grid=(1,), o...  13.1 us
    all_to_all x1, blocking collectives, shards(): lax.all_to_all(squares, 'opt', split_axis=0, concat_axis=0, tiled=True)  11.9 us
    pallas_call x2, Pallas kernels, directions(): pl.pallas_call(direction_kernel, grid_spec=grid_spec, out_shape=[jax.Shap...  9.77 us
    reshape x2, local copies, waits for them, and re-layouts, raw(): return got.reshape((SIDE, blocks, half_rows, width))  6.19 us
    add x2, other arithmetic, total(): return own + one + (three + two)  5.7 us
    all_to_all x1, waiting for transfers between devices, shards(): lax.all_to_all(squares, 'opt', split_axis=0, concat_axis=0, tiled=True)  4.97 us
  transfers between devices with their start and end apart: 48, of which 18 were waited for; matrix products, arithmetic and copies ran while one was open for 13% of the time, Pallas kernels for 11%

profile of v1, /device:TPU:0, one launch (start us, length us, event | category | flops | bytes accessed | tf_op | source)
XLA Modules:
  0.0 226.5 jit_solution(13306995793780200144)
XLA Ops:
  8.0 3.1 %dynamic-slice_bitcast_fusion = (bf16[4,6,32,512]{3,2,1,0:T(8,128)(2,1)}, bf16[4,6,32,512]{3,2,1,0:T(8,128)(2,1)}, bf16[4,6,32,512]{3,2,1,0:T(8,128)(2,1)}) fusion(bf16[4,4,6,64,512]{4,3,2,1,0:T(8,128)(2,1)} %bitcast.179, s32[]{:T(128)S(6)} %select_n.200, s32[]{:T(128)S(6)} %select_n.196, s32[]{:T(128)S(6)} %select_n.192), kind=kLoop, calls=%fused_computation.2 | loop fusion | bytes 4718604 | tf_op jit(solution)/shard_map/reshape | solution.py:63
  11.1 2.0 collective-permute-start.1
  13.1 2.1 collective-permute-start.3
  15.2 3.1 %dynamic-slice_bitcast_fusion.1 = (bf16[4,6,32,512]{3,2,1,0:T(8,128)(2,1)}, bf16[4,6,32,512]{3,2,1,0:T(8,128)(2,1)}, bf16[4,6,32,512]{3,2,1,0:T(8,128)(2,1)}) fusion(bf16[4,4,6,64,512]{4,3,2,1,0:T(8,128)(2,1)} %bitcast.180, s32[]{:T(128)S(6)} %select_n.198, s32[]{:T(128)S(6)} %select_n.194, s32[]{:T(128)S(6)} %select_n.190), kind=kLoop, calls=%fused_computation.3 | loop fusion | bytes 4718604 | tf_op jit(solution)/shard_map/reshape | solution.py:63
  21.5 2.0 collective-permute-start.4
  23.5 9.5 %collective-permute-done.1 = bf16[4,6,32,512]{3,2,1,0:T(8,128)(2,1)} collective-permute-done((bf16[4,6,32,512]{3,2,1,0:T(8,128)(2,1)}, bf16[4,6,32,512]{3,2,1,0:T(8,128)(2,1)}, u32[]{:S(2)}, u32[]{:S(2)}) %collective-permute-start.1) | collective-permute-done | bytes 786464 | tf_op jit(solution)/shard_map/ppermute | solution.py:31
  35.7 4.3 %all-to-all-start = ((bf16[2,8,64,512]{3,2,0,1:T(8,128)(2,1)}), bf16[2,8,64,512]{3,2,0,1:T(8,128)(2,1)S(1)}, u32[]{:S(2)}, u32[]{:S(2)}) async-start(bf16[2,8,64,512]{3,2,0,1:T(8,128)(2,1)} %copy.26), calls=%async_computation | async-start | bytes 2097152 | tf_op jit(solution)/shard_map/all_to_all | solution.py:283
  40.6 16.4 %collective-permute-done.4 = bf16[4,6,32,512]{3,2,1,0:T(8,128)(2,1)} collective-permute-done((bf16[4,6,32,512]{3,2,1,0:T(8,128)(2,1)}, bf16[4,6,32,512]{3,2,1,0:T(8,128)(2,1)}, u32[]{:S(2)}, u32[]{:S(2)}) %collective-permute-start.4) | collective-permute-done | bytes 786464 | tf_op jit(solution)/shard_map/ppermute | solution.py:31
  56.9 3.1 %fusion.8 = (f32[3,32,512]{2,1,0:T(8,128)S(1)}, f32[3,32,512]{2,1,0:T(8,128)S(1)}, f32[3,32,512]{2,1,0:T(8,128)}, f32[3,32,512]{2,1,0:T(8,128)S(1)}, f32[3,32,51...) fusion(bf16[4,6,32,512]{3,2,1,0:T(8,128)(2,1)} %collective-perm, ...), kind=kLoop, calls=%fused_computation.36 | loop fusion | flops 3096576 | bytes 5308448 | tf_op jit(solution)/shard_map/add | solution.py:76
  61.0 1.7 collective-permute-start.6
  64.2 3.1 %collective-permute-start.9 = (f32[3,32,512]{2,1,0:T(8,128)S(1)}, f32[3,32,512]{2,1,0:T(8,128)}, u32[]{:S(2)}, u32[]{:S(2)}) collective-permute-start(f32[3,32,512]{2,1,0:T(8,128)S(1)} %get-tuple-element.133), channel_id=1, source_target_pairs={{0,96},{8,104},{16,112},{24,120},{32,0},{40,8},{48,16},{56,24},{64... | collective-permute-start | bytes 589832 | tf_op jit(solution)/shard_map/ppermute | solution.py:31
  69.6 2.0 collective-permute-done.6
  71.7 1.7 collective-permute-done.9
  73.4 2.0 collective-permute-done.11
  76.7 2.6 %fusion.9 = (f32[3,32,512]{2,1,0:T(8,128)}, f32[3,32,512]{2,1,0:T(8,128)}, f32[3,32,512]{2,1,0:T(8,128)}, f32[3,32,512]{2,1,0:T(8,128)S(1)}) fusion(bf16[4,6,32,512]{3,2,1,0:T(8,128)(2,1)} %collective-permute-done.5, s32[]{:T(128)S(6)} %select_n.198, bf16[4,6,32,512]{3,2,1,0:T(8,128)(2,1)} %collective-permute-done.3, ...), kind=kLoop, calls=%fused_computation.38 | loop fusion | flops 1523712 | bytes 2949140 | tf_op jit(solution)/shard_map/add | solution.py:76
  80.1 2.3 %collective-permute-start.16 = (f32[3,32,512]{2,1,0:T(8,128)}, f32[3,32,512]{2,1,0:T(8,128)S(1)}, u32[]{:S(2)}, u32[]{:S(2)}) collective-permute-start(f32[3,32,512]{2,1,0:T(8,128)} %get-tuple-element.84), channel_id=1, source_target_pairs={{0,16},{8,24},{16,0},{24,8},{32,48},{40,56},{48,32},{56,40},{64,80... | collective-permute-start | bytes 589832 | tf_op jit(solution)/shard_map/ppermute | solution.py:31
  82.5 2.4 %collective-permute-start.15 = (f32[3,32,512]{2,1,0:T(8,128)S(1)}, f32[3,32,512]{2,1,0:T(8,128)S(1)}, u32[]{:S(2)}, u32[]{:S(2)}) collective-permute-start(f32[3,32,512]{2,1,0:T(8,128)S(1)} %get-tuple-element.83), channel_id=1, source_target_pairs={{0,96},{8,104},{16,112},{24,120},{32,0},{40,8},{48,16},{56,24},{64... | collective-permute-start | bytes 589832 | tf_op jit(solution)/shard_map/ppermute | solution.py:31
  84.8 1.9 collective-permute-start.14
  88.8 3.7 %collective-permute-done.15 = f32[3,32,512]{2,1,0:T(8,128)S(1)} collective-permute-done((f32[3,32,512]{2,1,0:T(8,128)S(1)}, f32[3,32,512]{2,1,0:T(8,128)S(1)}, u32[]{:S(2)}, u32[]{:S(2)}) %collective-permute-start.15) | collective-permute-done | bytes 196640 | tf_op jit(solution)/shard_map/ppermute | solution.py:31
  95.8 2.5 %multiply_reduce_fusion = (f32[3]{0:T(128)S(1)}, f32[3]{0:T(128)S(1)}, f32[3,64,512]{2,1,0:T(8,128)}, f32[3,64,512]{2,1,0:T(8,128)}, bf16[3,64,512]{2,1,0:T(8,12...) fusion(f32[3,32,512]{2,1,0:T(8,128)S(1)} %get-tuple-element.143, ...), kind=kLoop, calls=%fused_computation.28 | loop fusion | flops 2457594 | bytes 2949144 | tf_op jit(solution)/shard_map/reduce_sum | solution.py:303
  98.2 5.0 %all-gather.8.cloned.1.call-done.grad_ref.refs_0_ = bf16[8,3,64,512]{3,2,1,0:T(8,128)(2,1)} async-done(((bf16[1,3,64,512]{3,2,1,0:T(8,128)(2,1)}), bf16[8,3,64,512]{3,2,1,0:T(8,128)(2,1)}) %all-gather.8.cloned.1.call-update) | async-done | bytes 1572880 | tf_op jit(solution)/shard_map/all_gather | solution.py:300
  105.8 5.0 %directions.2 = (f32[3,64,512]{2,1,0:T(8,128)}, f32[3,8,128]{2,1,0:T(8,128)}) custom-call(s32[3]{0:T(128)} %get-tuple-element.168.owner_ref, s32[3]{0:T(128)} %get-tuple-element.166.rank_ref, bf16[2,8,64,512]{3,2,1,0:T(8,128)(2,1)} %copy.27.left_ref, bf16[8,3,64,512]{3,2,1,0:T(8,128)(2,1)} %all-gather.8.cloned.1.call-done.grad_ref.refs_0_, ...), custom_call_target="tpu_custom_call" | custom-call | flops 201326592 | bytes 3145728 | tf_op jit(solution)/shard_map/directions/pallas_call | solution.py:159
  111.6 11.9 %all_to_all.15 = f32[8,6,8,128]{3,2,1,0:T(8,128)S(1)} all-to-all(f32[8,6,8,128]{3,2,1,0:T(8,128)S(1)} %broadcast_in_dim.21), channel_id=1, replica_groups=mesh['dp'=16,'opt'=8] {'opt'}, dimensions={0} | all-to-all | bytes 393216 | tf_op jit(solution)/shard_map/all_to_all | solution.py:310
  123.7 1.9 fusion.35
  128.7 1.8 collective-permute-start.20
  130.5 1.7 collective-permute-start.21
  132.1 1.8 collective-permute-start.22
  133.9 1.9 collective-permute-start.23
  135.9 2.4 %collective-permute-done.22 = bf16[3,32,512]{2,1,0:T(8,128)(2,1)S(1)} collective-permute-done((bf16[3,32,512]{2,1,0:T(8,128)(2,1)S(1)}, bf16[3,32,512]{2,1,0:T(8,128)(2,1)S(1)}, u32[]{:S(2)}, u32[]{:S(2)}) %collective-permute-start.22) | collective-permute-done | bytes 98336 | tf_op jit(solution)/shard_map/ppermute | solution.py:31
  138.3 1.8 collective-permute-done.23
  140.5 2.9 %collective-permute-start.27 = (bf16[4,3,32,512]{3,2,1,0:T(8,128)(2,1)S(1)}, bf16[4,3,32,512]{3,2,1,0:T(8,128)(2,1)S(1)}, u32[]{:S(2)}, u32[]{:S(2)}) collective-permute-start(bf16[4,3,32,512]{3,2,1,0:T(8,128)(2,1)S(1)} %pad_maximum_fusion.5.upper_ref), channel_id=1, source_target_pairs={{0,96},{8,104},{16,112},{24,120},{32,0},{40,8},{48,16},{56,24},{64... | collective-permute-start | bytes 1179656 | tf_op jit(solution)/shard_map/ppermute | solution.py:31
  144.1 2.6 %collective-permute-start.26 = (bf16[4,3,32,512]{3,2,1,0:T(8,128)(2,1)S(1)}, bf16[4,3,32,512]{3,2,1,0:T(8,128)(2,1)S(1)}, u32[]{:S(2)}, u32[]{:S(2)}) collective-permute-start(bf16[4,3,32,512]{3,2,1,0:T(8,128)(2,1)S(1)} %pad_maximum_fusion.4.lower_ref), channel_id=1, source_target_pairs={{0,24},{8,0},{16,8},{24,16},{32,56},{40,32},{48,40},{56,48},{64,88... | collective-permute-start | bytes 1179656 | tf_op jit(solution)/shard_map/ppermute | solution.py:31
  146.8 4.8 %directions.3 = (f32[3,64,512]{2,1,0:T(8,128)}, f32[3,8,128]{2,1,0:T(8,128)}) custom-call(s32[3]{0:T(128)} %get-tuple-element.169.owner_ref, s32[3]{0:T(128)} %get-tuple-element.167.rank_ref, bf16[2,8,64,512]{3,2,1,0:T(8,128)(2,1)} %copy.27.left_ref, bf16[8,3,64,512]{3,2,1,0:T(8,128)(2,1)} %bitcast.187, bf16[8,2,512,512]{3,2,1,0:T(8,128)(2,1)} %bitcast.178), custom_call_target="tpu_custom_call" | custom-call | flops 201326592 | bytes 3145728 | tf_op jit(solution)/shard_map/directions/pallas_call | solution.py:159
  153.1 3.4 %all-to-all-start.2 = ((f32[8,6,8,128]{3,2,1,0:T(8,128)}), f32[8,6,8,128]{3,2,1,0:T(8,128)S(1)}, u32[]{:S(2)}, u32[]{:S(2)}) async-start(f32[8,6,8,128]{3,2,1,0:T(8,128)} %broadcast_in_dim.23), calls=%async_computation.2 | async-start | bytes 393216 | tf_op jit(solution)/shard_map/all_to_all | solution.py:310
  156.5 1.7 pad_maximum_fusion.8
  158.3 5.0 %all-to-all-done.2 = f32[8,6,8,128]{3,2,1,0:T(8,128)S(1)} async-done(((f32[8,6,8,128]{3,2,1,0:T(8,128)}), f32[8,6,8,128]{3,2,1,0:T(8,128)S(1)}, u32[]{:S(2)}, u32[]{:S(2)}) %all-to-all-start.2) | async-done | bytes 196640 | tf_op jit(solution)/shard_map/all_to_all | solution.py:310
  164.8 3.2 %collective-permute-start.30 = (bf16[3,32,512]{2,1,0:T(8,128)(2,1)S(1)}, bf16[3,32,512]{2,1,0:T(8,128)(2,1)S(1)}, u32[]{:S(2)}, u32[]{:S(2)}) collective-permute-start(bf16[3,32,512]{2,1,0:T(8,128)(2,1)S(1)} %get-tuple-element.161), channel_id=1, source_target_pairs={{0,24},{8,0},{16,8},{24,16},{32,56},{40,32},{48,40},{56,48},{64,88... | collective-permute-start | bytes 294920 | tf_op jit(solution)/shard_map/ppermute | solution.py:31
  168.0 3.2 %collective-permute-start.31 = (bf16[3,32,512]{2,1,0:T(8,128)(2,1)S(1)}, bf16[3,32,512]{2,1,0:T(8,128)(2,1)S(1)}, u32[]{:S(2)}, u32[]{:S(2)}) collective-permute-start(bf16[3,32,512]{2,1,0:T(8,128)(2,1)S(1)} %get-tuple-element.105), channel_id=1, source_target_pairs={{0,96},{8,104},{16,112},{24,120},{32,0},{40,8},{48,16},{56,24},{64... | collective-permute-start | bytes 294920 | tf_op jit(solution)/shard_map/ppermute | solution.py:31
  171.2 3.6 %collective-permute-start.41 = (bf16[4,3,32,512]{3,2,1,0:T(8,128)(2,1)S(1)}, bf16[4,3,32,512]{3,2,1,0:T(8,128)(2,1)S(1)}, u32[]{:S(2)}, u32[]{:S(2)}) collective-permute-start(bf16[4,3,32,512]{3,2,1,0:T(8,128)(2,1)S(1)} %pad_maximum_fusion.4.lower_ref), channel_id=1, source_target_pairs={{0,16},{8,24},{16,0},{24,8},{32,48},{40,56},{48,32},{56,40},{64,80... | collective-permute-start | bytes 1179656 | tf_op jit(solution)/shard_map/ppermute | solution.py:31
  174.8 3.6 %collective-permute-done.32 = bf16[3,32,512]{2,1,0:T(8,128)(2,1)S(1)} collective-permute-done((bf16[3,32,512]{2,1,0:T(8,128)(2,1)S(1)}, bf16[3,32,512]{2,1,0:T(8,128)(2,1)S(1)}, u32[]{:S(2)}, u32[]{:S(2)}) %collective-permute-start.32) | collective-permute-done | bytes 98336 | tf_op jit(solution)/shard_map/ppermute | solution.py:31
  178.7 6.2 %collective-permute-start.40 = (bf16[4,3,32,512]{3,2,1,0:T(8,128)(2,1)S(1)}, bf16[4,3,32,512]{3,2,1,0:T(8,128)(2,1)S(1)}, u32[]{:S(2)}, u32[]{:S(2)}) collective-permute-start(bf16[4,3,32,512]{3,2,1,0:T(8,128)(2,1)S(1)} %pad_maximum_fusion.5.upper_ref), channel_id=1, source_target_pairs={{0,64},{8,72},{16,80},{24,88},{32,96},{40,104},{48,112},{56,120},{... | collective-permute-start | bytes 1179656 | tf_op jit(solution)/shard_map/ppermute | solution.py:31
  185.6 2.1 pad_maximum_fusion.1
  187.7 3.7 %collective-permute-start.38 = (bf16[4,3,32,512]{3,2,1,0:T(8,128)(2,1)S(1)}, bf16[4,3,32,512]{3,2,1,0:T(8,128)(2,1)}, u32[]{:S(2)}, u32[]{:S(2)}) collective-permute-start(bf16[4,3,32,512]{3,2,1,0:T(8,128)(2,1)S(1)} %pad_maximum_fusion.7.lower_ref), channel_id=1, source_target_pairs={{0,24},{8,0},{16,8},{24,16},{32,56},{40,32},{48,40},{56,48},{64,88... | collective-permute-start | bytes 1179656 | tf_op jit(solution)/shard_map/ppermute | solution.py:31
  191.3 8.3 %collective-permute-done.34.upper_ref = bf16[4,3,32,512]{3,2,1,0:T(8,128)(2,1)S(1)} collective-permute-done((bf16[4,3,32,512]{3,2,1,0:T(8,128)(2,1)S(1)}, bf16[4,3,32,512]{3,2,1,0:T(8,128)(2,1)S(1)}, u32[]{:S(2)}, u32[]{:S(2)}) %collective-permute-start.34) | collective-permute-done | bytes 393248 | tf_op jit(solution)/shard_map/ppermute | solution.py:31
  199.7 2.0 pad_maximum_fusion
  207.8 4.9 %factors.1 = (f32[1,1,2,512,512]{4,3,2,1,0:T(8,128)}, f32[1,1,2,512,512]{4,3,2,1,0:T(8,128)}) custom-call(s32[2]{0:T(128)} %get-tuple-element.122.block_ref, s32[2]{0:T(128)} %get-tuple-element.121.used_ref, bf16[8,3,64,512]{3,2,1,0:T(8,128)(2,1)} %all-gather.8.cloned.1.call-done.grad_ref.refs_0_, bf16[8,3,64,512]{3,2,1,0:T(8,128)(2,1)} %bitcast.188, ...), custom_call_target="tpu_custom_call" | custom-call | flops 3221225472 | bytes 10485760 | tf_op jit(solution)/shard_map/factors/pallas_call | solution.py:226
  215.7 2.1 place_weights.14.refs_0_
  217.8 2.1 place_weights.15
  (113 shorter events, 40.3 us)
Async XLA Ops:
  7.2 68.2 %all-gather.10.cloned.1.call-start = ((), (), s32[]{:S(2)}) async-start(), calls=%async_computation.4 | async-start | bytes 9437184 | tf_op jit(solution)/shard_map/all_gather | solution.py:282
  11.1 22.0 %collective-permute-start.1 = (bf16[4,6,32,512]{3,2,1,0:T(8,128)(2,1)}, bf16[4,6,32,512]{3,2,1,0:T(8,128)(2,1)}, u32[]{:S(2)}, u32[]{:S(2)}) collective-permute-start(bf16[4,6,32,512]{3,2,1,0:T(8,128)(2,1)} %get-tuple-element.149), channel_id=1, source_target_pairs={{0,32},{8,40},{16,48},{24,56},{32,64},{40,72},{48,80},{56,88},{64,... | collective-permute-start | bytes 2359304 | tf_op jit(solution)/shard_map/ppermute | solution.py:31
  13.1 27.0 %collective-permute-start.3 = (bf16[4,6,32,512]{3,2,1,0:T(8,128)(2,1)}, bf16[4,6,32,512]{3,2,1,0:T(8,128)(2,1)}, u32[]{:S(2)}, u32[]{:S(2)}) collective-permute-start(bf16[4,6,32,512]{3,2,1,0:T(8,128)(2,1)} %get-tuple-element.148), channel_id=1, source_target_pairs={{0,96},{8,104},{16,112},{24,120},{32,0},{40,8},{48,16},{56,24},{64... | collective-permute-start | bytes 2359304 | tf_op jit(solution)/shard_map/ppermute | solution.py:31
  18.3 21.8 %collective-permute-start = (bf16[4,6,32,512]{3,2,1,0:T(8,128)(2,1)}, bf16[4,6,32,512]{3,2,1,0:T(8,128)(2,1)S(1)}, u32[]{:S(2)}, u32[]{:S(2)}) collective-permute-start(bf16[4,6,32,512]{3,2,1,0:T(8,128)(2,1)} %get-tuple-element.152), channel_id=1, source_target_pairs={{0,8},{8,16},{16,24},{24,0},{32,40},{40,48},{48,56},{56,32},{64,72... | collective-permute-start | bytes 2359304 | tf_op jit(solution)/shard_map/ppermute | solution.py:31
  19.9 20.7 %collective-permute-start.2 = (bf16[4,6,32,512]{3,2,1,0:T(8,128)(2,1)}, bf16[4,6,32,512]{3,2,1,0:T(8,128)(2,1)S(1)}, u32[]{:S(2)}, u32[]{:S(2)}) collective-permute-start(bf16[4,6,32,512]{3,2,1,0:T(8,128)(2,1)} %get-tuple-element.151), channel_id=1, source_target_pairs={{0,24},{8,0},{16,8},{24,16},{32,56},{40,32},{48,40},{56,48},{64,88... | collective-permute-start | bytes 2359304 | tf_op jit(solution)/shard_map/ppermute | solution.py:31
  21.5 35.4 %collective-permute-start.4 = (bf16[4,6,32,512]{3,2,1,0:T(8,128)(2,1)}, bf16[4,6,32,512]{3,2,1,0:T(8,128)(2,1)}, u32[]{:S(2)}, u32[]{:S(2)}) collective-permute-start(bf16[4,6,32,512]{3,2,1,0:T(8,128)(2,1)} %get-tuple-element.150), channel_id=1, source_target_pairs={{0,16},{8,24},{16,0},{24,8},{32,48},{40,56},{48,32},{56,40},{64,80... | collective-permute-start | bytes 2359304 | tf_op jit(solution)/shard_map/ppermute | solution.py:31
  33.1 23.9 %collective-permute-start.5 = (bf16[4,6,32,512]{3,2,1,0:T(8,128)(2,1)}, bf16[4,6,32,512]{3,2,1,0:T(8,128)(2,1)}, u32[]{:S(2)}, u32[]{:S(2)}) collective-permute-start(bf16[4,6,32,512]{3,2,1,0:T(8,128)(2,1)} %get-tuple-element.62), channel_id=1, source_target_pairs={{0,64},{8,72},{16,80},{24,88},{32,96},{40,104},{48,112},{56,120},{... | collective-permute-start | bytes 2359304 | tf_op jit(solution)/shard_map/ppermute | solution.py:31
  35.7 39.6 %all-to-all-start = ((bf16[2,8,64,512]{3,2,0,1:T(8,128)(2,1)}), bf16[2,8,64,512]{3,2,0,1:T(8,128)(2,1)S(1)}, u32[]{:S(2)}, u32[]{:S(2)}) async-start(bf16[2,8,64,512]{3,2,0,1:T(8,128)(2,1)} %copy.26), calls=%async_computation | async-start | bytes 2097152 | tf_op jit(solution)/shard_map/all_to_all | solution.py:283
  40.0 63.2 %all-gather.8.cloned.1.call-start = ((), (), s32[]{:S(2)}) async-start(), calls=%async_computation.3 | async-start | bytes 1769472 | tf_op jit(solution)/shard_map/all_gather | solution.py:300
  60.0 7.4 %collective-permute-start.7 = (f32[3,32,512]{2,1,0:T(8,128)S(1)}, f32[3,32,512]{2,1,0:T(8,128)S(1)}, u32[]{:S(2)}, u32[]{:S(2)}) collective-permute-start(f32[3,32,512]{2,1,0:T(8,128)S(1)} %get-tuple-element.134), channel_id=1, source_target_pairs={{0,32},{8,40},{16,48},{24,56},{32,64},{40,72},{48,80},{56,88},{64,... | collective-permute-start | bytes 589832 | tf_op jit(solution)/shard_map/ppermute | solution.py:31
  60.1 9.5 %collective-permute-start.10 = (f32[3,32,512]{2,1,0:T(8,128)}, f32[3,32,512]{2,1,0:T(8,128)}, u32[]{:S(2)}, u32[]{:S(2)}) collective-permute-start(f32[3,32,512]{2,1,0:T(8,128)} %get-tuple-element.146), channel_id=1, source_target_pairs={{0,16},{8,24},{16,0},{24,8},{32,48},{40,56},{48,32},{56,40},{64,80... | collective-permute-start | bytes 589832 | tf_op jit(solution)/shard_map/ppermute | solution.py:31
  61.0 10.7 %collective-permute-start.6 = (f32[3,32,512]{2,1,0:T(8,128)}, f32[3,32,512]{2,1,0:T(8,128)}, u32[]{:S(2)}, u32[]{:S(2)}) collective-permute-start(f32[3,32,512]{2,1,0:T(8,128)} %get-tuple-element.144), channel_id=1, source_target_pairs={{0,8},{8,16},{16,24},{24,0},{32,40},{40,48},{48,56},{56,32},{64,72... | collective-permute-start | bytes 589832 | tf_op jit(solution)/shard_map/ppermute | solution.py:31
  62.7 8.9 %collective-permute-start.8 = (f32[3,32,512]{2,1,0:T(8,128)}, f32[3,32,512]{2,1,0:T(8,128)}, u32[]{:S(2)}, u32[]{:S(2)}) collective-permute-start(f32[3,32,512]{2,1,0:T(8,128)} %get-tuple-element.145), channel_id=1, source_target_pairs={{0,24},{8,0},{16,8},{24,16},{32,56},{40,32},{48,40},{56,48},{64,88... | collective-permute-start | bytes 589832 | tf_op jit(solution)/shard_map/ppermute | solution.py:31
  64.2 9.1 %collective-permute-start.9 = (f32[3,32,512]{2,1,0:T(8,128)S(1)}, f32[3,32,512]{2,1,0:T(8,128)}, u32[]{:S(2)}, u32[]{:S(2)}) collective-permute-start(f32[3,32,512]{2,1,0:T(8,128)S(1)} %get-tuple-element.133), channel_id=1, source_target_pairs={{0,96},{8,104},{16,112},{24,120},{32,0},{40,8},{48,16},{56,24},{64... | collective-permute-start | bytes 589832 | tf_op jit(solution)/shard_map/ppermute | solution.py:31
  68.1 7.3 %collective-permute-start.11 = (f32[3,32,512]{2,1,0:T(8,128)S(1)}, f32[3,32,512]{2,1,0:T(8,128)}, u32[]{:S(2)}, u32[]{:S(2)}) collective-permute-start(f32[3,32,512]{2,1,0:T(8,128)S(1)} %get-tuple-element.69), channel_id=1, source_target_pairs={{0,64},{8,72},{16,80},{24,88},{32,96},{40,104},{48,112},{56,120},{... | collective-permute-start | bytes 589832 | tf_op jit(solution)/shard_map/ppermute | solution.py:31
  80.0 66.8 %all-gather.12.cloned.1.call-start = ((), (), s32[]{:S(2)}) async-start(), calls=%async_computation.5 | async-start | bytes 1769472 | tf_op jit(solution)/shard_map/all_gather | solution.py:300
  80.1 7.2 %collective-permute-start.13 = (f32[3,32,512]{2,1,0:T(8,128)}, f32[3,32,512]{2,1,0:T(8,128)S(1)}, u32[]{:S(2)}, u32[]{:S(2)}) collective-permute-start(f32[3,32,512]{2,1,0:T(8,128)} %get-tuple-element.81), channel_id=1, source_target_pairs={{0,32},{8,40},{16,48},{24,56},{32,64},{40,72},{48,80},{56,88},{64,... | collective-permute-start | bytes 589832 | tf_op jit(solution)/shard_map/ppermute | solution.py:31
  80.1 8.6 %collective-permute-start.16 = (f32[3,32,512]{2,1,0:T(8,128)}, f32[3,32,512]{2,1,0:T(8,128)S(1)}, u32[]{:S(2)}, u32[]{:S(2)}) collective-permute-start(f32[3,32,512]{2,1,0:T(8,128)} %get-tuple-element.84), channel_id=1, source_target_pairs={{0,16},{8,24},{16,0},{24,8},{32,48},{40,56},{48,32},{56,40},{64,80... | collective-permute-start | bytes 589832 | tf_op jit(solution)/shard_map/ppermute | solution.py:31
  82.5 10.0 %collective-permute-start.15 = (f32[3,32,512]{2,1,0:T(8,128)S(1)}, f32[3,32,512]{2,1,0:T(8,128)S(1)}, u32[]{:S(2)}, u32[]{:S(2)}) collective-permute-start(f32[3,32,512]{2,1,0:T(8,128)S(1)} %get-tuple-element.83), channel_id=1, source_target_pairs={{0,96},{8,104},{16,112},{24,120},{32,0},{40,8},{48,16},{56,24},{64... | collective-permute-start | bytes 589832 | tf_op jit(solution)/shard_map/ppermute | solution.py:31
  84.8 7.7 %collective-permute-start.14 = (f32[3,32,512]{2,1,0:T(8,128)}, f32[3,32,512]{2,1,0:T(8,128)S(1)}, u32[]{:S(2)}, u32[]{:S(2)}) collective-permute-start(f32[3,32,512]{2,1,0:T(8,128)} %get-tuple-element.82), channel_id=1, source_target_pairs={{0,24},{8,0},{16,8},{24,16},{32,56},{40,32},{48,40},{56,48},{64,88... | collective-permute-start | bytes 589832 | tf_op jit(solution)/shard_map/ppermute | solution.py:31
  86.7 7.1 %collective-permute-start.12 = (f32[3,32,512]{2,1,0:T(8,128)}, f32[3,32,512]{2,1,0:T(8,128)S(1)}, u32[]{:S(2)}, u32[]{:S(2)}) collective-permute-start(f32[3,32,512]{2,1,0:T(8,128)} %get-tuple-element.80), channel_id=1, source_target_pairs={{0,8},{8,16},{16,24},{24,0},{32,40},{40,48},{48,56},{56,32},{64,72... | collective-permute-start | bytes 589832 | tf_op jit(solution)/shard_map/ppermute | solution.py:31
  87.2 7.2 %collective-permute-start.17 = (f32[3,32,512]{2,1,0:T(8,128)S(1)}, f32[3,32,512]{2,1,0:T(8,128)S(1)}, u32[]{:S(2)}, u32[]{:S(2)}) collective-permute-start(f32[3,32,512]{2,1,0:T(8,128)S(1)} %get-tuple-element.86), channel_id=1, source_target_pairs={{0,64},{8,72},{16,80},{24,88},{32,96},{40,104},{48,112},{56,120},{... | collective-permute-start | bytes 589832 | tf_op jit(solution)/shard_map/ppermute | solution.py:31
  125.6 8.3 %collective-permute-start.19 = (bf16[3,32,512]{2,1,0:T(8,128)(2,1)S(1)}, bf16[3,32,512]{2,1,0:T(8,128)(2,1)S(1)}, u32[]{:S(2)}, u32[]{:S(2)}) collective-permute-start(bf16[3,32,512]{2,1,0:T(8,128)(2,1)S(1)} %get-tuple-element.96), channel_id=1, source_target_pairs={{0,32},{8,40},{16,48},{24,56},{32,64},{40,72},{48,80},{56,88},{64,... | collective-permute-start | bytes 294920 | tf_op jit(solution)/shard_map/ppermute | solution.py:31
  127.2 8.7 %collective-permute-start.18 = (bf16[3,32,512]{2,1,0:T(8,128)(2,1)S(1)}, bf16[3,32,512]{2,1,0:T(8,128)(2,1)S(1)}, u32[]{:S(2)}, u32[]{:S(2)}) collective-permute-start(bf16[3,32,512]{2,1,0:T(8,128)(2,1)S(1)} %get-tuple-element.165), channel_id=1, source_target_pairs={{0,8},{8,16},{16,24},{24,0},{32,40},{40,48},{48,56},{56,32},{64,72... | collective-permute-start | bytes 294920 | tf_op jit(solution)/shard_map/ppermute | solution.py:31
  128.7 7.2 %collective-permute-start.20 = (bf16[3,32,512]{2,1,0:T(8,128)(2,1)S(1)}, bf16[3,32,512]{2,1,0:T(8,128)(2,1)S(1)}, u32[]{:S(2)}, u32[]{:S(2)}) collective-permute-start(bf16[3,32,512]{2,1,0:T(8,128)(2,1)S(1)} %get-tuple-element.165), channel_id=1, source_target_pairs={{0,24},{8,0},{16,8},{24,16},{32,56},{40,32},{48,40},{56,48},{64,88... | collective-permute-start | bytes 294920 | tf_op jit(solution)/shard_map/ppermute | solution.py:31
  130.5 5.4 %collective-permute-start.21 = (bf16[3,32,512]{2,1,0:T(8,128)(2,1)S(1)}, bf16[3,32,512]{2,1,0:T(8,128)(2,1)S(1)}, u32[]{:S(2)}, u32[]{:S(2)}) collective-permute-start(bf16[3,32,512]{2,1,0:T(8,128)(2,1)S(1)} %get-tuple-element.96), channel_id=1, source_target_pairs={{0,96},{8,104},{16,112},{24,120},{32,0},{40,8},{48,16},{56,24},{64... | collective-permute-start | bytes 294920 | tf_op jit(solution)/shard_map/ppermute | solution.py:31
  132.1 6.1 %collective-permute-start.22 = (bf16[3,32,512]{2,1,0:T(8,128)(2,1)S(1)}, bf16[3,32,512]{2,1,0:T(8,128)(2,1)S(1)}, u32[]{:S(2)}, u32[]{:S(2)}) collective-permute-start(bf16[3,32,512]{2,1,0:T(8,128)(2,1)S(1)} %get-tuple-element.165), channel_id=1, source_target_pairs={{0,16},{8,24},{16,0},{24,8},{32,48},{40,56},{48,32},{56,40},{64,80... | collective-permute-start | bytes 294920 | tf_op jit(solution)/shard_map/ppermute | solution.py:31
  133.9 6.1 %collective-permute-start.23 = (bf16[3,32,512]{2,1,0:T(8,128)(2,1)S(1)}, bf16[3,32,512]{2,1,0:T(8,128)(2,1)S(1)}, u32[]{:S(2)}, u32[]{:S(2)}) collective-permute-start(bf16[3,32,512]{2,1,0:T(8,128)(2,1)S(1)} %get-tuple-element.96), channel_id=1, source_target_pairs={{0,64},{8,72},{16,80},{24,88},{32,96},{40,104},{48,112},{56,120},{... | collective-permute-start | bytes 294920 | tf_op jit(solution)/shard_map/ppermute | solution.py:31
  140.1 18.1 %collective-permute-start.25 = (bf16[4,3,32,512]{3,2,1,0:T(8,128)(2,1)S(1)}, bf16[4,3,32,512]{3,2,1,0:T(8,128)(2,1)S(1)}, u32[]{:S(2)}, u32[]{:S(2)}) collective-permute-start(bf16[4,3,32,512]{3,2,1,0:T(8,128)(2,1)S(1)} %pad_maximum_fusion.5.upper_ref), channel_id=1, source_target_pairs={{0,32},{8,40},{16,48},{24,56},{32,64},{40,72},{48,80},{56,88},{64,... | collective-permute-start | bytes 1179656 | tf_op jit(solution)/shard_map/ppermute | solution.py:31
  140.5 17.7 %collective-permute-start.27 = (bf16[4,3,32,512]{3,2,1,0:T(8,128)(2,1)S(1)}, bf16[4,3,32,512]{3,2,1,0:T(8,128)(2,1)S(1)}, u32[]{:S(2)}, u32[]{:S(2)}) collective-permute-start(bf16[4,3,32,512]{3,2,1,0:T(8,128)(2,1)S(1)} %pad_maximum_fusion.5.upper_ref), channel_id=1, source_target_pairs={{0,96},{8,104},{16,112},{24,120},{32,0},{40,8},{48,16},{56,24},{64... | collective-permute-start | bytes 1179656 | tf_op jit(solution)/shard_map/ppermute | solution.py:31
  143.5 14.8 %collective-permute-start.24 = (bf16[4,3,32,512]{3,2,1,0:T(8,128)(2,1)S(1)}, bf16[4,3,32,512]{3,2,1,0:T(8,128)(2,1)S(1)}, u32[]{:S(2)}, u32[]{:S(2)}) collective-permute-start(bf16[4,3,32,512]{3,2,1,0:T(8,128)(2,1)S(1)} %pad_maximum_fusion.4.lower_ref), channel_id=1, source_target_pairs={{0,8},{8,16},{16,24},{24,0},{32,40},{40,48},{48,56},{56,32},{64,72... | collective-permute-start | bytes 1179656 | tf_op jit(solution)/shard_map/ppermute | solution.py:31
  144.1 14.1 %collective-permute-start.26 = (bf16[4,3,32,512]{3,2,1,0:T(8,128)(2,1)S(1)}, bf16[4,3,32,512]{3,2,1,0:T(8,128)(2,1)S(1)}, u32[]{:S(2)}, u32[]{:S(2)}) collective-permute-start(bf16[4,3,32,512]{3,2,1,0:T(8,128)(2,1)S(1)} %pad_maximum_fusion.4.lower_ref), channel_id=1, source_target_pairs={{0,24},{8,0},{16,8},{24,16},{32,56},{40,32},{48,40},{56,48},{64,88... | collective-permute-start | bytes 1179656 | tf_op jit(solution)/shard_map/ppermute | solution.py:31
  153.1 10.2 %all-to-all-start.2 = ((f32[8,6,8,128]{3,2,1,0:T(8,128)}), f32[8,6,8,128]{3,2,1,0:T(8,128)S(1)}, u32[]{:S(2)}, u32[]{:S(2)}) async-start(f32[8,6,8,128]{3,2,1,0:T(8,128)} %broadcast_in_dim.23), calls=%async_computation.2 | async-start | bytes 393216 | tf_op jit(solution)/shard_map/all_to_all | solution.py:310
  156.5 51.3 %all-gather.14.cloned.1.call-start = ((), (), s32[]{:S(2)}) async-start(), calls=%async_computation.6 | async-start | bytes 3538944 | tf_op jit(solution)/shard_map/all_gather | solution.py:320
  164.6 6.5 %collective-permute-start.29 = (bf16[3,32,512]{2,1,0:T(8,128)(2,1)S(1)}, bf16[3,32,512]{2,1,0:T(8,128)(2,1)S(1)}, u32[]{:S(2)}, u32[]{:S(2)}) collective-permute-start(bf16[3,32,512]{2,1,0:T(8,128)(2,1)S(1)} %get-tuple-element.105), channel_id=1, source_target_pairs={{0,32},{8,40},{16,48},{24,56},{32,64},{40,72},{48,80},{56,88},{64,... | collective-permute-start | bytes 294920 | tf_op jit(solution)/shard_map/ppermute | solution.py:31
  164.7 6.5 %collective-permute-start.28 = (bf16[3,32,512]{2,1,0:T(8,128)(2,1)S(1)}, bf16[3,32,512]{2,1,0:T(8,128)(2,1)S(1)}, u32[]{:S(2)}, u32[]{:S(2)}) collective-permute-start(bf16[3,32,512]{2,1,0:T(8,128)(2,1)S(1)} %get-tuple-element.161), channel_id=1, source_target_pairs={{0,8},{8,16},{16,24},{24,0},{32,40},{40,48},{48,56},{56,32},{64,72... | collective-permute-start | bytes 294920 | tf_op jit(solution)/shard_map/ppermute | solution.py:31
  164.8 10.0 %collective-permute-start.30 = (bf16[3,32,512]{2,1,0:T(8,128)(2,1)S(1)}, bf16[3,32,512]{2,1,0:T(8,128)(2,1)S(1)}, u32[]{:S(2)}, u32[]{:S(2)}) collective-permute-start(bf16[3,32,512]{2,1,0:T(8,128)(2,1)S(1)} %get-tuple-element.161), channel_id=1, source_target_pairs={{0,24},{8,0},{16,8},{24,16},{32,56},{40,32},{48,40},{56,48},{64,88... | collective-permute-start | bytes 294920 | tf_op jit(solution)/shard_map/ppermute | solution.py:31
  168.0 6.8 %collective-permute-start.31 = (bf16[3,32,512]{2,1,0:T(8,128)(2,1)S(1)}, bf16[3,32,512]{2,1,0:T(8,128)(2,1)S(1)}, u32[]{:S(2)}, u32[]{:S(2)}) collective-permute-start(bf16[3,32,512]{2,1,0:T(8,128)(2,1)S(1)} %get-tuple-element.105), channel_id=1, source_target_pairs={{0,96},{8,104},{16,112},{24,120},{32,0},{40,8},{48,16},{56,24},{64... | collective-permute-start | bytes 294920 | tf_op jit(solution)/shard_map/ppermute | solution.py:31
  171.1 7.2 %collective-permute-start.32 = (bf16[3,32,512]{2,1,0:T(8,128)(2,1)S(1)}, bf16[3,32,512]{2,1,0:T(8,128)(2,1)S(1)}, u32[]{:S(2)}, u32[]{:S(2)}) collective-permute-start(bf16[3,32,512]{2,1,0:T(8,128)(2,1)S(1)} %get-tuple-element.161), channel_id=1, source_target_pairs={{0,16},{8,24},{16,0},{24,8},{32,48},{40,56},{48,32},{56,40},{64,80... | collective-permute-start | bytes 294920 | tf_op jit(solution)/shard_map/ppermute | solution.py:31
  171.1 7.2 %collective-permute-start.33 = (bf16[3,32,512]{2,1,0:T(8,128)(2,1)S(1)}, bf16[3,32,512]{2,1,0:T(8,128)(2,1)S(1)}, u32[]{:S(2)}, u32[]{:S(2)}) collective-permute-start(bf16[3,32,512]{2,1,0:T(8,128)(2,1)S(1)} %get-tuple-element.105), channel_id=1, source_target_pairs={{0,64},{8,72},{16,80},{24,88},{32,96},{40,104},{48,112},{56,120},{... | collective-permute-start | bytes 294920 | tf_op jit(solution)/shard_map/ppermute | solution.py:31
  171.2 28.4 %collective-permute-start.41 = (bf16[4,3,32,512]{3,2,1,0:T(8,128)(2,1)S(1)}, bf16[4,3,32,512]{3,2,1,0:T(8,128)(2,1)S(1)}, u32[]{:S(2)}, u32[]{:S(2)}) collective-permute-start(bf16[4,3,32,512]{3,2,1,0:T(8,128)(2,1)S(1)} %pad_maximum_fusion.4.lower_ref), channel_id=1, source_target_pairs={{0,16},{8,24},{16,0},{24,8},{32,48},{40,56},{48,32},{56,40},{64,80... | collective-permute-start | bytes 1179656 | tf_op jit(solution)/shard_map/ppermute | solution.py:31
  178.4 21.2 %collective-permute-start.34 = (bf16[4,3,32,512]{3,2,1,0:T(8,128)(2,1)S(1)}, bf16[4,3,32,512]{3,2,1,0:T(8,128)(2,1)S(1)}, u32[]{:S(2)}, u32[]{:S(2)}) collective-permute-start(bf16[4,3,32,512]{3,2,1,0:T(8,128)(2,1)S(1)} %pad_maximum_fusion.6.upper_ref), channel_id=1, source_target_pairs={{0,32},{8,40},{16,48},{24,56},{32,64},{40,72},{48,80},{56,88},{64,... | collective-permute-start | bytes 1179656 | tf_op jit(solution)/shard_map/ppermute | solution.py:31
  178.6 21.0 %collective-permute-start.39 = (bf16[4,3,32,512]{3,2,1,0:T(8,128)(2,1)S(1)}, bf16[4,3,32,512]{3,2,1,0:T(8,128)(2,1)S(1)}, u32[]{:S(2)}, u32[]{:S(2)}) collective-permute-start(bf16[4,3,32,512]{3,2,1,0:T(8,128)(2,1)S(1)} %pad_maximum_fusion.7.lower_ref), channel_id=1, source_target_pairs={{0,8},{8,16},{16,24},{24,0},{32,40},{40,48},{48,56},{56,32},{64,72... | collective-permute-start | bytes 1179656 | tf_op jit(solution)/shard_map/ppermute | solution.py:31
  178.7 27.6 %collective-permute-start.40 = (bf16[4,3,32,512]{3,2,1,0:T(8,128)(2,1)S(1)}, bf16[4,3,32,512]{3,2,1,0:T(8,128)(2,1)S(1)}, u32[]{:S(2)}, u32[]{:S(2)}) collective-permute-start(bf16[4,3,32,512]{3,2,1,0:T(8,128)(2,1)S(1)} %pad_maximum_fusion.5.upper_ref), channel_id=1, source_target_pairs={{0,64},{8,72},{16,80},{24,88},{32,96},{40,104},{48,112},{56,120},{... | collective-permute-start | bytes 1179656 | tf_op jit(solution)/shard_map/ppermute | solution.py:31
  187.7 28.1 %collective-permute-start.38 = (bf16[4,3,32,512]{3,2,1,0:T(8,128)(2,1)S(1)}, bf16[4,3,32,512]{3,2,1,0:T(8,128)(2,1)}, u32[]{:S(2)}, u32[]{:S(2)}) collective-permute-start(bf16[4,3,32,512]{3,2,1,0:T(8,128)(2,1)S(1)} %pad_maximum_fusion.7.lower_ref), channel_id=1, source_target_pairs={{0,24},{8,0},{16,8},{24,16},{32,56},{40,32},{48,40},{56,48},{64,88... | collective-permute-start | bytes 1179656 | tf_op jit(solution)/shard_map/ppermute | solution.py:31
  199.6 16.1 %collective-permute-start.37 = (bf16[4,3,32,512]{3,2,1,0:T(8,128)(2,1)S(1)}, bf16[4,3,32,512]{3,2,1,0:T(8,128)(2,1)}, u32[]{:S(2)}, u32[]{:S(2)}) collective-permute-start(bf16[4,3,32,512]{3,2,1,0:T(8,128)(2,1)S(1)} %pad_maximum_fusion.6.upper_ref), channel_id=1, source_target_pairs={{0,96},{8,104},{16,112},{24,120},{32,0},{40,8},{48,16},{56,24},{64... | collective-permute-start | bytes 1179656 | tf_op jit(solution)/shard_map/ppermute | solution.py:31
  199.6 18.2 %collective-permute-start.36 = (bf16[4,3,32,512]{3,2,1,0:T(8,128)(2,1)S(1)}, bf16[4,3,32,512]{3,2,1,0:T(8,128)(2,1)}, u32[]{:S(2)}, u32[]{:S(2)}) collective-permute-start(bf16[4,3,32,512]{3,2,1,0:T(8,128)(2,1)S(1)} %pad_maximum_fusion.7.lower_ref), channel_id=1, source_target_pairs={{0,16},{8,24},{16,0},{24,8},{32,48},{40,56},{48,32},{56,40},{64,80... | collective-permute-start | bytes 1179656 | tf_op jit(solution)/shard_map/ppermute | solution.py:31
  199.6 18.2 %collective-permute-start.35 = (bf16[4,3,32,512]{3,2,1,0:T(8,128)(2,1)S(1)}, bf16[4,3,32,512]{3,2,1,0:T(8,128)(2,1)}, u32[]{:S(2)}, u32[]{:S(2)}) collective-permute-start(bf16[4,3,32,512]{3,2,1,0:T(8,128)(2,1)S(1)} %pad_maximum_fusion.6.upper_ref), channel_id=1, source_target_pairs={{0,64},{8,72},{16,80},{24,88},{32,96},{40,104},{48,112},{56,120},{... | collective-permute-start | bytes 1179656 | tf_op jit(solution)/shard_map/ppermute | solution.py:31
  (6 other events, 95.8 us)
Sparse Core Ops, SparseCore 0:
  9.7 63.3 all-gather.9
  80.1 22.9 all-gather.7
  104.9 25.7 all-gather.11
  163.4 22.2 all-gather.13

commit v2 on v1

v2 whole, which is shorter than its diff:
```python
import functools

import jax
import jax.numpy as jnp
from jax import lax
from jax.experimental import pallas as pl
from jax.experimental.pallas import tpu as pltpu
from jax.sharding import PartitionSpec as P

BETA_FACTOR = 0.75
BETA_MOMENT = 0.95
LEARN_RATE = 0.1
EPS_ADAM = 1e-08
EPS_GRAFT = 1e-06
SIDE = 4
VMEM = 60 * 2**20


def shift_perm(axis, step):
    pairs = []
    for z in range(SIDE):
        for y in range(SIDE):
            to_z = (z + step) % SIDE if axis == "z" else z
            to_y = (y + step) % SIDE if axis == "y" else y
            pairs.append((z * SIDE + y, to_z * SIDE + to_y))
    return pairs


def send(value, axis, step):
    return lax.ppermute(value, "dp", shift_perm(axis, step))


def after(value, *earlier):
    return lax.optimization_barrier((value,) + earlier)[0]


ORDER = (("y", 1), ("z", 1), ("y", 3), ("z", 3), ("y", 2), ("z", 2))
OTHER = {"y": "z", "z": "y"}


def exchange(make):
    got = {}
    for axis, step in ORDER:
        value = make(axis, step)
        got[axis, step] = send(after(value, got["z", 1]) if (axis, step) == ORDER[-1] else value, axis, step)
    return got


def together(got):
    return dict(zip(got, lax.optimization_barrier(tuple(got.values()))))


def sum_replicas(parts, place, needed):
    blocks, half_rows, width = parts.shape[2], parts.shape[3] // 2, parts.shape[4]
    top = {"y": 0, "z": half_rows}

    def raw(axis, step):
        at = (place[axis] + step) % SIDE
        start = (0, at, 0, top[axis], 0) if axis == "y" else (at, 0, 0, top[axis], 0)
        size = (SIDE, 1) if axis == "y" else (1, SIDE)
        got = lax.dynamic_slice(parts, start, size + (blocks, half_rows, width))
        return got.reshape((SIDE, blocks, half_rows, width))

    near = together(exchange(raw))

    def total(axis, step):
        at = (place[axis] + step) % SIDE
        axis = OTHER[axis]
        start = (at, place["y"]) if axis == "y" else (place["z"], at)
        own = lax.dynamic_slice(parts, start + (0, top[axis], 0), (1, 1, blocks, half_rows, width))[0, 0]
        picked = [lax.dynamic_index_in_dim(near[axis, hop], at, 0, keepdims=False) for hop in (1, 3, 2)]
        own, one, three, two = [part.astype(jnp.float32) for part in [own] + picked]
        return (own + one) + (three + two)

    far = together(exchange(total))
    halves = []
    for axis in ("y", "z"):
        one, three, two = [far[OTHER[axis], step] for step in (1, 3, 2)]
        halves.append((total(OTHER[axis], 0) + one) + (after(three, *needed) + two))
    return jnp.concatenate(halves, axis=1)


def place_kernel(step, place_ref, *refs):
    out, sems = refs[-2:]
    pieces = refs[:-2]
    z, y = place_ref[0], place_ref[1]
    still_z, still_y = lax.rem(z + SIDE - step, SIDE), lax.rem(y + SIDE - step, SIDE)
    count = pieces[0].shape[0]
    rows = pieces[0].shape[2]
    copies = []
    for hop in range(SIDE):
        upper = out.at[still_z, lax.rem(y + SIDE - hop, SIDE), :, pl.ds(0, rows)]
        lower = out.at[lax.rem(z + SIDE - hop, SIDE), still_y, :, pl.ds(rows, rows)]
        for half, target in enumerate((upper, lower)):
            source = pieces[half * (SIDE // count) + hop // count].at[hop % count]
            copies.append(pltpu.make_async_copy(source, target, sems.at[half * SIDE + hop]))
    for copy in copies:
        copy.start()
    for copy in copies:
        copy.wait()


def put(out, shape, place, step, upper, lower):
    spot = jnp.stack([place["z"], place["y"]]).astype(jnp.int32)
    before = [] if out is None else [out]
    pieces = upper + lower
    piece = pl.BlockSpec(pieces[0].shape, lambda t: (0, 0, 0, 0))

    def kernel(place_ref, *refs):
        place_kernel(step, place_ref, *refs[: len(pieces)], *refs[-2:])

    return pl.pallas_call(
        kernel,
        grid=(1,),
        out_shape=jax.ShapeDtypeStruct(shape, jnp.bfloat16),
        in_specs=[pl.BlockSpec(memory_space=pltpu.SMEM)]
        + [piece] * len(pieces)
        + [pl.BlockSpec(memory_space=pl.ANY)] * len(before),
        out_specs=pl.BlockSpec(memory_space=pl.ANY),
        scratch_shapes=[pltpu.SemaphoreType.DMA((2 * SIDE,))],
        input_output_aliases={1 + len(pieces): 0} if before else {},
        compiler_params=pltpu.CompilerParams(vmem_limit_bytes=8 * 2**20),
        cost_estimate=pl.CostEstimate(
            flops=0, bytes_accessed=4 * sum(value.size for value in pieces), transcendentals=0
        ),
        name="place_weights",
    )(spot, *pieces, *before)


def direction_kernel(owner_ref, rank_ref, left_ref, grad_ref, right_ref, adam_ref, out_ref, square_ref):
    k = pl.program_id(0)
    width = right_ref.shape[-1]
    grad = grad_ref[...].reshape(width, width)
    half = jnp.dot(left_ref[0, 0], grad, preferred_element_type=jnp.float32).astype(jnp.bfloat16)
    rows = jnp.dot(half, right_ref[0, 0], preferred_element_type=jnp.float32)
    out_ref[0] = rows

    @pl.when(k == 0)
    def _():
        square_ref[...] = adam_ref[...]

    lane = lax.broadcasted_iota(jnp.int32, square_ref.shape, 1)
    square_ref[...] += jnp.where(lane == k, jnp.sum(rows * rows), 0.0)


def directions(owner, rank, left_rows, grad_whole, right_roots, adam_square):
    opt_count, blocks, slab_rows, width = grad_whole.shape
    grid_spec = pltpu.PrefetchScalarGridSpec(
        num_scalar_prefetch=2,
        grid=(blocks,),
        in_specs=[
            pl.BlockSpec((1, 1, slab_rows, width), lambda k, owner, rank: (rank[k], owner[k], 0, 0)),
            pl.BlockSpec((opt_count, 1, slab_rows, width), lambda k, owner, rank: (0, k, 0, 0)),
            pl.BlockSpec((1, 1, width, width), lambda k, owner, rank: (owner[k], rank[k], 0, 0)),
            pl.BlockSpec((8, 128), lambda k, owner, rank: (0, 0)),
        ],
        out_specs=[
            pl.BlockSpec((1, slab_rows, width), lambda k, owner, rank: (k, 0, 0)),
            pl.BlockSpec((8, 128), lambda k, owner, rank: (0, 0)),
        ],
    )
    flops = blocks * 4 * slab_rows * width * width
    return pl.pallas_call(
        direction_kernel,
        grid_spec=grid_spec,
        out_shape=[
            jax.ShapeDtypeStruct((blocks, slab_rows, width), jnp.float32),
            jax.ShapeDtypeStruct((8, 128), jnp.float32),
        ],
        compiler_params=pltpu.CompilerParams(vmem_limit_bytes=VMEM),
        cost_estimate=pl.CostEstimate(
            flops=flops, bytes_accessed=blocks * width * width * 4, transcendentals=0
        ),
        name="directions",
    )(owner, rank, left_rows, grad_whole, right_roots, adam_square)


def gram_kernel(block_ref, used_ref, high_ref, low_ref, left_ref, right_ref, left_out, right_out):
    slot = pl.program_id(0)
    width = left_ref.shape[-1]

    @pl.when(used_ref[slot] == 1)
    def _():
        high = high_ref[...].reshape(width, width)
        low = low_ref[...].reshape(width, width)
        scale = (1.0 - BETA_FACTOR) / width

        def gram(dims):
            dot = functools.partial(
                lax.dot_general, dimension_numbers=(dims, ((), ())), preferred_element_type=jnp.float32
            )
            cross = dot(high, low)
            return dot(high, high) + (cross + cross.T)

        left_out[0, 0, 0] = BETA_FACTOR * left_ref[0, 0, 0] + scale * gram(((1,), (1,)))
        right_out[0, 0, 0] = BETA_FACTOR * right_ref[0, 0, 0] + scale * gram(((0,), (0,)))

    @pl.when(used_ref[slot] == 0)
    def _():
        left_out[...] = left_ref[...]
        right_out[...] = right_ref[...]


def factors(block_at, used, high, low, factor_left, factor_right):
    slot_count, width = factor_left.shape[2], factor_left.shape[-1]
    opt_count, _, slab_rows, _ = high.shape
    grad_spec = pl.BlockSpec((opt_count, 1, slab_rows, width), lambda s, at, used: (0, at[s], 0, 0))
    state_spec = pl.BlockSpec((1, 1, 1, width, width), lambda s, at, used: (0, 0, s, 0, 0))
    grid_spec = pltpu.PrefetchScalarGridSpec(
        num_scalar_prefetch=2,
        grid=(slot_count,),
        in_specs=[grad_spec, grad_spec, state_spec, state_spec],
        out_specs=[state_spec, state_spec],
    )
    return pl.pallas_call(
        gram_kernel,
        grid_spec=grid_spec,
        out_shape=[jax.ShapeDtypeStruct(factor_left.shape, jnp.float32)] * 2,
        compiler_params=pltpu.CompilerParams(vmem_limit_bytes=VMEM),
        cost_estimate=pl.CostEstimate(
            flops=slot_count * 12 * width**3,
            bytes_accessed=slot_count * 20 * width * width,
            transcendentals=0,
        ),
        name="factors",
    )(block_at, used, high, low, factor_left, factor_right)


def gather_weights(weights, shape, place, meanwhile):
    half_rows = weights.shape[1] // 2
    own = {"y": weights[:, :half_rows], "z": weights[:, half_rows:]}
    near = together(exchange(lambda axis, step: own[axis]))
    line = {axis: jnp.stack([own[axis]] + [near[axis, hop] for hop in (1, 2, 3)]) for axis in own}
    far = {(axis, step): send(line[OTHER[axis]], axis, step) for axis, step in ORDER[:4]}
    for axis in ("y", "z"):
        halves = [send(far[axis, 1][:2], axis, 1), send(far[axis, 3][2:], axis, 3)]
        far[axis, 2] = halves
    out = put(None, shape, place, 0, [line["y"]], [line["z"]])
    out = put(out, shape, place, 1, [far["z", 1]], [far["y", 1]])
    far["z", 3] = after(far["z", 3], meanwhile)
    out = put(out, shape, place, 3, [far["z", 3]], [far["y", 3]])
    return put(out, shape, place, 2, far["z", 2], far["y", 2])


def shards(
    grad_partial,
    master,
    second_moment,
    owner_table,
    factor_left,
    factor_right,
    root_left,
    root_right,
):
    opt_count = lax.axis_size("opt")
    slot_count = factor_left.shape[2]
    row_blocks, slab_rows, width = master.shape
    dp_at, opt_at = lax.axis_index("dp"), lax.axis_index("opt")
    place = {"z": dp_at // SIDE, "y": dp_at % SIDE}

    owner = lax.dynamic_slice_in_dim(owner_table[:, 0], dp_at * row_blocks, row_blocks, 0)
    position = jnp.arange(row_blocks)
    same_owner = owner[:, None] == owner[None, :]
    earlier = position[None, :] < position[:, None]
    rank = jnp.sum((same_owner & earlier).astype(jnp.int32), axis=1)
    mine = (owner[None, :] == opt_at) & (rank[None, :] == jnp.arange(slot_count)[:, None])
    used = jnp.sum(mine.astype(jnp.int32), axis=1)
    block_at = jnp.sum(jnp.where(mine, position[None, :], 0), axis=1).astype(jnp.int32)

    right_roots = lax.all_gather(root_right[0, 0], "opt", axis=0)
    left_rows = lax.all_to_all(
        root_left[0, 0].reshape(slot_count, opt_count, slab_rows, width),
        "opt",
        split_axis=1,
        concat_axis=1,
        tiled=True,
    )

    parts = grad_partial[0].reshape(SIDE, SIDE, row_blocks, slab_rows, width)
    grad = sum_replicas(parts, place, (left_rows, right_roots))

    rounded = lax.reduce_precision(grad, 8, 7)
    high = rounded.astype(jnp.bfloat16)
    high_whole = lax.all_gather(high, "opt", axis=0)
    moment_new = BETA_MOMENT * second_moment + (1.0 - BETA_MOMENT) * grad * grad
    step = grad / (jnp.sqrt(moment_new) + EPS_ADAM)
    adam_square = jnp.sum(step * step, axis=(1, 2))
    adam_tile = jnp.pad(adam_square[None], ((0, 7), (64, 64 - row_blocks)))
    rows, squares = directions(owner, rank, left_rows, high_whole, right_roots, adam_tile)
    squares = jnp.broadcast_to(squares[None], (opt_count,) + squares.shape)
    squares = lax.all_to_all(squares, "opt", split_axis=0, concat_axis=0, tiled=True)
    totals = jnp.sum(squares[:, 0], axis=0)
    row_total, adam_total = totals[:row_blocks], totals[64 : 64 + row_blocks]
    graft_scale = jnp.sqrt(adam_total) / (jnp.sqrt(row_total) + EPS_GRAFT)
    master_new = master - LEARN_RATE * graft_scale[:, None, None] * rows

    low = after((grad - rounded).astype(jnp.bfloat16), squares)
    low_whole = lax.all_gather(low, "opt", axis=0)
    left_new, right_new = factors(block_at, used, high_whole, low_whole, factor_left, factor_right)
    weights = gather_weights(master_new.astype(jnp.bfloat16), parts.shape, place, left_new)
    return (master_new, moment_new, weights.reshape(-1, slab_rows, width), left_new, right_new)


def solution(mesh):
    placed = (
        P("dp", None, "opt", None),
        P("dp", "opt", None),
        P("dp", "opt", None),
        P(),
        P("dp", "opt", None, None, None),
        P("dp", "opt", None, None, None),
        P("dp", "opt", None, None, None),
        P("dp", "opt", None, None, None),
    )
    return jax.shard_map(
        shards,
        mesh=mesh,
        in_specs=placed,
        out_specs=(
            P("dp", "opt", None),
            P("dp", "opt", None),
            P(None, "opt", None),
            P("dp", "opt", None, None, None),
            P("dp", "opt", None, None, None),
        ),
        check_vma=False,
    )
```

time: 229 us -> 196 us (0.86)
  starting transfers between devices: 71.4 us -> 46.5 us
  waiting for transfers between devices: 66.6 us -> 80.9 us
  other arithmetic: 23.4 us -> 13.4 us
  Pallas kernels: 27.8 us -> 20.3 us
  blocking collectives: 11.9 us -> 8.27 us
    ppermute x42 -> x26, starting transfers between devices: 63.6 us -> 42.1 us  [send(): return lax.ppermute(value, 'dp', shift_perm(axis, step))]
    all_gather x3 -> x2, waiting for transfers between devices: 4.99 us -> 23.3 us  [the longest x1 23.3 us: shards(): high_whole = lax.all_gather(high, 'opt', axis=0)]
    concatenate x5 -> x0, other arithmetic: 7.35 us -> none  [the longest x1 2.08 us: shards(): jnp.concatenate(moments, axis=0)]
    pallas_call x8 -> x4, Pallas kernels: 13.1 us -> 7 us  [put(): pl.pallas_call(kernel, grid=(1,), out_shape=jax.ShapeDtypeStruct(shape, j...]
    all_to_all x1 -> x0, waiting for transfers between devices: 4.97 us -> none  [shards(): lax.all_to_all(squares, 'opt', split_axis=0, concat_axis=0, tiled=True)]
    all_to_all x1, blocking collectives: 11.9 us -> 8.27 us  [shards(): lax.all_to_all(squares, 'opt', split_axis=0, concat_axis=0, tiled=True)]
    all_to_all x1 -> x0, starting transfers between devices: 3.39 us -> none  [shards(): lax.all_to_all(squares, 'opt', split_axis=0, concat_axis=0, tiled=True)]
    pallas_call x2 -> x1, Pallas kernels: 9.77 us -> 7.39 us  [directions(): pl.pallas_call(direction_kernel, grid_spec=grid_spec, out_shape=[jax.Shap...]
  transfers between devices with their start and end apart: 48 -> 30, of which waited for: 18 -> 13; matrix products, arithmetic and copies ran while one was open for 13% -> 11% of each run, Pallas kernels for 11% -> 6%
where the time goes in v2:
time: 196 us
  waiting for transfers between devices  80.9 us (41%)
  starting transfers between devices  46.5 us (24%)
  Pallas kernels  20.3 us (10%)
  between operations  14.1 us (7%)
  other arithmetic  13.4 us (7%)
  local copies, waits for them, and re-layouts  12.2 us (6%)
  blocking collectives  8.27 us (4%)
    ppermute x26, waiting for transfers between devices, send(): return lax.ppermute(value, 'dp', shift_perm(axis, step))  56.9 us
    ppermute x26, starting transfers between devices, send(): return lax.ppermute(value, 'dp', shift_perm(axis, step))  42.1 us
    all_gather x1, waiting for transfers between devices, shards(): high_whole = lax.all_gather(high, 'opt', axis=0)  23.3 us
    all_to_all x1, blocking collectives, shards(): lax.all_to_all(squares, 'opt', split_axis=0, concat_axis=0, tiled=True)  8.27 us
    pallas_call x1, Pallas kernels, directions(): pl.pallas_call(direction_kernel, grid_spec=grid_spec, out_shape=[jax.Shap...  7.39 us
    pallas_call x4, Pallas kernels, put(): pl.pallas_call(kernel, grid=(1,), out_shape=jax.ShapeDtypeStruct(shape, j...  7 us
    reshape x2, local copies, waits for them, and re-layouts, raw(): return got.reshape((SIDE, blocks, half_rows, width))  6.19 us
    pallas_call x1, Pallas kernels, factors(): pl.pallas_call(gram_kernel, grid_spec=grid_spec, out_shape=[jax.ShapeDtyp...  5.95 us
  transfers between devices with their start and end apart: 30, of which 13 were waited for; matrix products, arithmetic and copies ran while one was open for 11% of the time, Pallas kernels for 6%

profile of v2, /device:TPU:0, one launch (start us, length us, event | category | flops | bytes accessed | tf_op | source)
XLA Modules:
  0.0 195.7 jit_solution(15054962896611351176)
XLA Ops:
  8.0 3.1 %dynamic-slice_bitcast_fusion = (bf16[4,6,32,512]{3,2,1,0:T(8,128)(2,1)}, bf16[4,6,32,512]{3,2,1,0:T(8,128)(2,1)}, bf16[4,6,32,512]{3,2,1,0:T(8,128)(2,1)}) fusion(bf16[4,4,6,64,512]{4,3,2,1,0:T(8,128)(2,1)} %bitcast.102, s32[]{:T(128)S(6)} %select_n.146, s32[]{:T(128)S(6)} %select_n.142, s32[]{:T(128)S(6)} %select_n.138), kind=kLoop, calls=%fused_computation.11 | loop fusion | bytes 4718604 | tf_op jit(solution)/shard_map/reshape | solution.py:62
  11.1 2.0 %collective-permute-start.1 = (bf16[4,6,32,512]{3,2,1,0:T(8,128)(2,1)}, bf16[4,6,32,512]{3,2,1,0:T(8,128)(2,1)S(1)}, u32[]{:S(2)}, u32[]{:S(2)}) collective-permute-start(bf16[4,6,32,512]{3,2,1,0:T(8,128)(2,1)} %get-tuple-element.84), channel_id=1, source_target_pairs={{0,32},{8,40},{16,48},{24,56},{32,64},{40,72},{48,80},{56,88},{64,... | collective-permute-start | bytes 2359304 | tf_op jit(solution)/shard_map/ppermute | solution.py:30
  13.1 2.1 %collective-permute-start.3 = (bf16[4,6,32,512]{3,2,1,0:T(8,128)(2,1)}, bf16[4,6,32,512]{3,2,1,0:T(8,128)(2,1)S(1)}, u32[]{:S(2)}, u32[]{:S(2)}) collective-permute-start(bf16[4,6,32,512]{3,2,1,0:T(8,128)(2,1)} %get-tuple-element.83), channel_id=1, source_target_pairs={{0,96},{8,104},{16,112},{24,120},{32,0},{40,8},{48,16},{56,24},{64... | collective-permute-start | bytes 2359304 | tf_op jit(solution)/shard_map/ppermute | solution.py:30
  15.2 3.1 %dynamic-slice_bitcast_fusion.1 = (bf16[4,6,32,512]{3,2,1,0:T(8,128)(2,1)}, bf16[4,6,32,512]{3,2,1,0:T(8,128)(2,1)}, bf16[4,6,32,512]{3,2,1,0:T(8,128)(2,1)}) fusion(bf16[4,4,6,64,512]{4,3,2,1,0:T(8,128)(2,1)} %bitcast.103, s32[]{:T(128)S(6)} %select_n.144, s32[]{:T(128)S(6)} %select_n.140, s32[]{:T(128)S(6)} %select_n.136), kind=kLoop, calls=%fused_computation.12 | loop fusion | bytes 4718604 | tf_op jit(solution)/shard_map/reshape | solution.py:62
  18.3 1.6 collective-permute-start
  19.9 1.7 collective-permute-start.2
  21.5 2.0 %collective-permute-start.4 = (bf16[4,6,32,512]{3,2,1,0:T(8,128)(2,1)}, bf16[4,6,32,512]{3,2,1,0:T(8,128)(2,1)}, u32[]{:S(2)}, u32[]{:S(2)}) collective-permute-start(bf16[4,6,32,512]{3,2,1,0:T(8,128)(2,1)} %get-tuple-element.85), channel_id=1, source_target_pairs={{0,16},{8,24},{16,0},{24,8},{32,48},{40,56},{48,32},{56,40},{64,80... | collective-permute-start | bytes 2359304 | tf_op jit(solution)/shard_map/ppermute | solution.py:30
  23.5 9.4 %collective-permute-done.1 = bf16[4,6,32,512]{3,2,1,0:T(8,128)(2,1)S(1)} collective-permute-done((bf16[4,6,32,512]{3,2,1,0:T(8,128)(2,1)}, bf16[4,6,32,512]{3,2,1,0:T(8,128)(2,1)S(1)}, u32[]{:S(2)}, u32[]{:S(2)}) %collective-permute-start.1) | collective-permute-done | bytes 786464 | tf_op jit(solution)/shard_map/ppermute | solution.py:30
  33.0 1.6 collective-permute-start.5
  34.5 1.1 copy.22
  35.6 4.3 %all-to-all-start = ((bf16[2,8,64,512]{3,2,0,1:T(8,128)(2,1)}), bf16[2,8,64,512]{3,2,0,1:T(8,128)(2,1)S(1)}, u32[]{:S(2)}, u32[]{:S(2)}) async-start(bf16[2,8,64,512]{3,2,0,1:T(8,128)(2,1)} %copy.22), calls=%async_computation | async-start | bytes 2097152 | tf_op jit(solution)/shard_map/all_to_all | solution.py:271
  40.7 16.2 %collective-permute-done.4 = bf16[4,6,32,512]{3,2,1,0:T(8,128)(2,1)} collective-permute-done((bf16[4,6,32,512]{3,2,1,0:T(8,128)(2,1)}, bf16[4,6,32,512]{3,2,1,0:T(8,128)(2,1)}, u32[]{:S(2)}, u32[]{:S(2)}) %collective-permute-start.4) | collective-permute-done | bytes 786464 | tf_op jit(solution)/shard_map/ppermute | solution.py:30
  56.9 3.5 %fusion.6 = (f32[6,32,512]{2,1,0:T(8,128)}, f32[6,32,512]{2,1,0:T(8,128)}, f32[6,32,512]{2,1,0:T(8,128)S(1)}, f32[6,32,512]{2,1,0:T(8,128)}, f32[6,32,512]{2,1,0:T(8,128)}, /*index=5*/f32[6,32,512]{2,1,0:T(8,128)}) fusion(bf16[4,6,32,512]{3,2,1,0:T(8,128)(2,1)} %collective-permute-done.4, s32[]{:T(128)S(6)} %select_n.146, ...), kind=kLoop, calls=%fused_computation.22 | loop fusion | flops 4128768 | bytes 7077920 | tf_op jit(solution)/shard_map/add | solution.py:73
  60.5 1.1 collective-permute-start.10
  61.6 1.6 collective-permute-start.6
  63.2 1.6 collective-permute-start.8
  64.8 3.2 %collective-permute-start.9 = (f32[6,32,512]{2,1,0:T(8,128)}, f32[6,32,512]{2,1,0:T(8,128)}, u32[]{:S(2)}, u32[]{:S(2)}) collective-permute-start(f32[6,32,512]{2,1,0:T(8,128)} %get-tuple-element.72), channel_id=1, source_target_pairs={{0,96},{8,104},{16,112},{24,120},{32,0},{40,8},{48,16},{56,24},{64... | collective-permute-start | bytes 1179656 | tf_op jit(solution)/shard_map/ppermute | solution.py:30
  68.0 3.5 %collective-permute-done.7 = f32[6,32,512]{2,1,0:T(8,128)} collective-permute-done((f32[6,32,512]{2,1,0:T(8,128)S(1)}, f32[6,32,512]{2,1,0:T(8,128)}, u32[]{:S(2)}, u32[]{:S(2)}) %collective-permute-start.7) | collective-permute-done | bytes 393248 | tf_op jit(solution)/shard_map/ppermute | solution.py:30
  71.5 2.9 %collective-permute-done.10 = f32[6,32,512]{2,1,0:T(8,128)} collective-permute-done((f32[6,32,512]{2,1,0:T(8,128)}, f32[6,32,512]{2,1,0:T(8,128)}, u32[]{:S(2)}, u32[]{:S(2)}) %collective-permute-start.10) | collective-permute-done | bytes 393248 | tf_op jit(solution)/shard_map/ppermute | solution.py:30
  74.4 6.1 %collective-permute-done.6 = f32[6,32,512]{2,1,0:T(8,128)} collective-permute-done((f32[6,32,512]{2,1,0:T(8,128)}, f32[6,32,512]{2,1,0:T(8,128)}, u32[]{:S(2)}, u32[]{:S(2)}) %collective-permute-start.6) | collective-permute-done | bytes 393248 | tf_op jit(solution)/shard_map/ppermute | solution.py:30
  80.5 1.9 collective-permute-done.9
  82.4 2.4 %fusion.14 = (f32[6,32,512]{2,1,0:T(8,128)S(1)}, f32[6,32,512]{2,1,0:T(8,128)S(1)}) fusion(f32[6,32,512]{2,1,0:T(8,128)} %collective-permute-done.7, f32[6,32,512]{2,1,0:T(8,128)} %collective-permute-done.9, f32[6,32,512]{2,1,0:T(8,128)} %collective-permute-done.11, bf16[4,6,32,512]{3,2,1,0:T(8,128)(2,1)} %collective-permute-done.4, s32[]{:T(128)S(6)} %select_n.132, ...), kind=kLoop, calls=%fused_computation.36 | loop fusion | flops 1966080 | bytes 4718608 | tf_op jit(solution)/shard_map/add | solution.py:79
  87.6 2.5 %multiply_reduce_fusion = (f32[6]{0:T(128)S(1)}, f32[6,64,512]{2,1,0:T(8,128)}, bf16[6,64,512]{2,1,0:T(8,128)(2,1)}) fusion(f32[6,32,512]{2,1,0:T(8,128)S(1)} %get-tuple-element.78, f32[6,32,512]{2,1,0:T(8,128)S(1)} %get-tuple-element.77, f32[6,64,512]{2,1,0:T(8,128)} %param.10), kind=kLoop, calls=%fused_computation.10 | loop fusion | flops 2359290 | bytes 2752536 | tf_op jit(solution)/shard_map/reduce_sum | solution.py:287
  90.8 23.3 %all-gather.6.cloned.1.call-done.grad_ref.high_ref = bf16[8,6,64,512]{3,2,1,0:T(8,128)(2,1)} async-done(((bf16[1,6,64,512]{3,2,1,0:T(8,128)(2,1)}), bf16[8,6,64,512]{3,2,1,0:T(8,128)(2,1)}) %all-gather.6.cloned.1.call-update) | async-done | bytes 3145744 | tf_op jit(solution)/shard_map/all_gather | solution.py:284
  114.1 7.4 %directions.1 = (f32[6,64,512]{2,1,0:T(8,128)}, f32[8,128]{1,0:T(8,128)}) custom-call(s32[6]{0:T(128)} %copy-done.3, s32[6]{0:T(128)} %convert_reduce_fusion.rank_ref, bf16[2,8,64,512]{3,2,1,0:T(8,128)(2,1)} %copy.23.left_ref, bf16[8,6,64,512]{3,2,1,0:T(8,128)(2,1)} %all-gather.6.cloned.1.call-done.grad_ref.high_ref, bf16[8,2,512,512]{3,2,1,0:T(8,128)(2,1)} %bitcast.101, ...), custom_call_target="tpu_custom_call" | custom-call | flops 402653184 | bytes 6291456 | tf_op jit(solution)/shard_map/directions/pallas_call | solution.py:163
  122.2 8.3 %all_to_all.10 = f32[8,8,128]{2,1,0:T(8,128)S(1)} all-to-all(f32[8,8,128]{2,1,0:T(8,128)S(1)} %broadcast_in_dim.17), channel_id=1, replica_groups=mesh['dp'=16,'opt'=8] {'opt'}, dimensions={0} | all-to-all | bytes 65536 | tf_op jit(solution)/shard_map/all_to_all | solution.py:291
  130.6 2.3 %fusion.19 = (bf16[6,64,512]{2,1,0:T(8,128)(2,1)S(1)}, f32[6,64,512]{2,1,0:T(8,128)}) fusion(f32[6,64,512]{2,1,0:T(8,128)S(1)} %copy-done.2, f32[6,64,512]{2,1,0:T(8,128)} %get-tuple-element.51, f32[6]{0:T(128)S(1)} %fusion.17), kind=kLoop, calls=%fused_computation.51 | loop fusion | flops 589824 | bytes 2752536 | tf_op jit(solution)/shard_map/convert_element_type | solution.py:300
  132.9 1.6 collective-permute-start.13
  134.5 1.5 collective-permute-start.12
  136.0 1.8 collective-permute-start.14
  137.8 1.7 collective-permute-start.15
  139.5 1.8 collective-permute-start.16
  141.3 1.9 collective-permute-start.17
  143.2 2.4 %collective-permute-done.14 = bf16[6,32,512]{2,1,0:T(8,128)(2,1)S(1)} collective-permute-done((bf16[6,32,512]{2,1,0:T(8,128)(2,1)S(1)}, bf16[6,32,512]{2,1,0:T(8,128)(2,1)S(1)}, u32[]{:S(2)}, u32[]{:S(2)}) %collective-permute-start.14) | collective-permute-done | bytes 196640 | tf_op jit(solution)/shard_map/ppermute | solution.py:30
  145.6 1.5 collective-permute-done.15
  147.2 1.2 collective-permute-done.17
  148.5 1.1 collective-permute-start.22
  149.6 2.2 %collective-permute-start.24 = (bf16[4,6,32,512]{3,2,1,0:T(8,128)(2,1)S(1)}, bf16[4,6,32,512]{3,2,1,0:T(8,128)(2,1)S(1)}, u32[]{:S(2)}, u32[]{:S(2)}) collective-permute-start(bf16[4,6,32,512]{3,2,1,0:T(8,128)(2,1)S(1)} %pad_maximum_fusion.2.refs_1_), channel_id=1, source_target_pairs={{0,24},{8,0},{16,8},{24,16},{32,56},{40,32},{48,40},{56,48},{64,88... | collective-permute-start | bytes 2359304 | tf_op jit(solution)/shard_map/ppermute | solution.py:30
  152.0 1.6 collective-permute-start.18
  153.6 1.7 collective-permute-start.20
  155.9 10.9 %collective-permute-done.22.refs_1_ = bf16[4,6,32,512]{3,2,1,0:T(8,128)(2,1)S(1)} collective-permute-done((bf16[4,6,32,512]{3,2,1,0:T(8,128)(2,1)S(1)}, bf16[4,6,32,512]{3,2,1,0:T(8,128)(2,1)S(1)}, u32[]{:S(2)}, u32[]{:S(2)}) %collective-permute-start.22) | collective-permute-done | bytes 786464 | tf_op jit(solution)/shard_map/ppermute | solution.py:30
  168.0 3.2 %collective-permute-start.25 = (bf16[2,6,32,512]{3,2,1,0:T(8,128)(2,1)}, bf16[2,6,32,512]{3,2,1,0:T(8,128)(2,1)S(1)}, u32[]{:S(2)}, u32[]{:S(2)}) collective-permute-start(bf16[2,6,32,512]{3,2,1,0:T(8,128)(2,1)} %slice.42), channel_id=1, source_target_pairs={{0,24},{8,0},{16,8},{24,16},{32,56},{40,32},{48,40},{56,48},{64,88... | collective-permute-start | bytes 1179656 | tf_op jit(solution)/shard_map/ppermute | solution.py:30
  172.0 2.4 %collective-permute-start.19 = (bf16[2,6,32,512]{3,2,1,0:T(8,128)(2,1)}, bf16[2,6,32,512]{3,2,1,0:T(8,128)(2,1)S(1)}, u32[]{:S(2)}, u32[]{:S(2)}) collective-permute-start(bf16[2,6,32,512]{3,2,1,0:T(8,128)(2,1)} %slice.39), channel_id=1, source_target_pairs={{0,32},{8,40},{16,48},{24,56},{32,64},{40,72},{48,80},{56,88},{64,... | collective-permute-start | bytes 1179656 | tf_op jit(solution)/shard_map/ppermute | solution.py:30
  176.1 1.7 place_weights.4.refs_2_
  177.8 1.8 place_weights.5.refs_2_
  179.6 6.0 %factors.1 = (f32[1,1,2,512,512]{4,3,2,1,0:T(8,128)}, f32[1,1,2,512,512]{4,3,2,1,0:T(8,128)}) custom-call(s32[2]{0:T(128)} %get-tuple-element.64.block_ref, s32[2]{0:T(128)} %get-tuple-element.63.used_ref, bf16[8,6,64,512]{3,2,1,0:T(8,128)(2,1)} %all-gather.6.cloned.1.call-done.grad_ref.high_ref, bf16[8,6,64,512]{3,2,1,0:T(8,128)(2,1)} %bitcast.117, ...), custom_call_target="tpu_custom_call" | custom-call | flops 3221225472 | bytes 10485760 | tf_op jit(solution)/shard_map/factors/pallas_call | solution.py:215
  185.6 1.7 place_weights.6.refs_4_
  187.4 1.8 place_weights.7
  (59 shorter events, 10.4 us)
Async XLA Ops:
  7.2 27.4 %copy-start = (bf16[1,1,2,512,512]{4,3,2,1,0:T(8,128)(2,1)S(1)}, bf16[1,1,2,512,512]{4,3,2,1,0:T(8,128)(2,1)}, u32[]{:S(2)}) copy-start(bf16[1,1,2,512,512]{4,3,2,1,0:T(8,128)(2,1)} %param.14) | copy-start | bytes 3145732
  7.2 75.3 %all-gather.8.cloned.1.call-start = ((), (), s32[]{:S(2)}) async-start(), calls=%async_computation.3 | async-start | bytes 9437184 | tf_op jit(solution)/shard_map/all_gather | solution.py:270
  11.1 21.9 %collective-permute-start.1 = (bf16[4,6,32,512]{3,2,1,0:T(8,128)(2,1)}, bf16[4,6,32,512]{3,2,1,0:T(8,128)(2,1)S(1)}, u32[]{:S(2)}, u32[]{:S(2)}) collective-permute-start(bf16[4,6,32,512]{3,2,1,0:T(8,128)(2,1)} %get-tuple-element.84), channel_id=1, source_target_pairs={{0,32},{8,40},{16,48},{24,56},{32,64},{40,72},{48,80},{56,88},{64,... | collective-permute-start | bytes 2359304 | tf_op jit(solution)/shard_map/ppermute | solution.py:30
  13.1 26.9 %collective-permute-start.3 = (bf16[4,6,32,512]{3,2,1,0:T(8,128)(2,1)}, bf16[4,6,32,512]{3,2,1,0:T(8,128)(2,1)S(1)}, u32[]{:S(2)}, u32[]{:S(2)}) collective-permute-start(bf16[4,6,32,512]{3,2,1,0:T(8,128)(2,1)} %get-tuple-element.83), channel_id=1, source_target_pairs={{0,96},{8,104},{16,112},{24,120},{32,0},{40,8},{48,16},{56,24},{64... | collective-permute-start | bytes 2359304 | tf_op jit(solution)/shard_map/ppermute | solution.py:30
  18.3 21.7 %collective-permute-start = (bf16[4,6,32,512]{3,2,1,0:T(8,128)(2,1)}, bf16[4,6,32,512]{3,2,1,0:T(8,128)(2,1)S(1)}, u32[]{:S(2)}, u32[]{:S(2)}) collective-permute-start(bf16[4,6,32,512]{3,2,1,0:T(8,128)(2,1)} %get-tuple-element.87), channel_id=1, source_target_pairs={{0,8},{8,16},{16,24},{24,0},{32,40},{40,48},{48,56},{56,32},{64,72... | collective-permute-start | bytes 2359304 | tf_op jit(solution)/shard_map/ppermute | solution.py:30
  19.9 20.8 %collective-permute-start.2 = (bf16[4,6,32,512]{3,2,1,0:T(8,128)(2,1)}, bf16[4,6,32,512]{3,2,1,0:T(8,128)(2,1)}, u32[]{:S(2)}, u32[]{:S(2)}) collective-permute-start(bf16[4,6,32,512]{3,2,1,0:T(8,128)(2,1)} %get-tuple-element.86), channel_id=1, source_target_pairs={{0,24},{8,0},{16,8},{24,16},{32,56},{40,32},{48,40},{56,48},{64,88... | collective-permute-start | bytes 2359304 | tf_op jit(solution)/shard_map/ppermute | solution.py:30
  21.5 35.4 %collective-permute-start.4 = (bf16[4,6,32,512]{3,2,1,0:T(8,128)(2,1)}, bf16[4,6,32,512]{3,2,1,0:T(8,128)(2,1)}, u32[]{:S(2)}, u32[]{:S(2)}) collective-permute-start(bf16[4,6,32,512]{3,2,1,0:T(8,128)(2,1)} %get-tuple-element.85), channel_id=1, source_target_pairs={{0,16},{8,24},{16,0},{24,8},{32,48},{40,56},{48,32},{56,40},{64,80... | collective-permute-start | bytes 2359304 | tf_op jit(solution)/shard_map/ppermute | solution.py:30
  33.0 24.0 %collective-permute-start.5 = (bf16[4,6,32,512]{3,2,1,0:T(8,128)(2,1)}, bf16[4,6,32,512]{3,2,1,0:T(8,128)(2,1)}, u32[]{:S(2)}, u32[]{:S(2)}) collective-permute-start(bf16[4,6,32,512]{3,2,1,0:T(8,128)(2,1)} %get-tuple-element.34), channel_id=1, source_target_pairs={{0,64},{8,72},{16,80},{24,88},{32,96},{40,104},{48,112},{56,120},{... | collective-permute-start | bytes 2359304 | tf_op jit(solution)/shard_map/ppermute | solution.py:30
  35.6 46.8 %all-to-all-start = ((bf16[2,8,64,512]{3,2,0,1:T(8,128)(2,1)}), bf16[2,8,64,512]{3,2,0,1:T(8,128)(2,1)S(1)}, u32[]{:S(2)}, u32[]{:S(2)}) async-start(bf16[2,8,64,512]{3,2,0,1:T(8,128)(2,1)} %copy.22), calls=%async_computation | async-start | bytes 2097152 | tf_op jit(solution)/shard_map/all_to_all | solution.py:271
  39.9 74.2 %all-gather.6.cloned.1.call-start = ((), (), s32[]{:S(2)}) async-start(), calls=%async_computation.2 | async-start | bytes 3538944 | tf_op jit(solution)/shard_map/all_gather | solution.py:284
  40.0 45.8 %copy-start.5 = (s32[96,1]{0,1:T(1,128)S(1)}, s32[96,1]{0,1:T(1,128)}, u32[]{:S(2)}) copy-start(s32[96,1]{0,1:T(1,128)} %param.11) | copy-start | bytes 1156
  40.0 42.4 %copy-start.1 = (bf16[4,6,32,512]{3,2,1,0:T(8,128)(2,1)}, bf16[4,6,32,512]{3,2,1,0:T(8,128)(2,1)S(1)}, u32[]{:S(2)}) copy-start(bf16[4,6,32,512]{3,2,1,0:T(8,128)(2,1)S(1)} %collective-permute-done) | copy-start | bytes 2359300
  60.5 11.0 %collective-permute-start.7 = (f32[6,32,512]{2,1,0:T(8,128)S(1)}, f32[6,32,512]{2,1,0:T(8,128)}, u32[]{:S(2)}, u32[]{:S(2)}) collective-permute-start(f32[6,32,512]{2,1,0:T(8,128)S(1)} %get-tuple-element.73), channel_id=1, source_target_pairs={{0,32},{8,40},{16,48},{24,56},{32,64},{40,72},{48,80},{56,88},{64,... | collective-permute-start | bytes 1179656 | tf_op jit(solution)/shard_map/ppermute | solution.py:30
  60.5 14.0 %collective-permute-start.10 = (f32[6,32,512]{2,1,0:T(8,128)}, f32[6,32,512]{2,1,0:T(8,128)}, u32[]{:S(2)}, u32[]{:S(2)}) collective-permute-start(f32[6,32,512]{2,1,0:T(8,128)} %get-tuple-element.81), channel_id=1, source_target_pairs={{0,16},{8,24},{16,0},{24,8},{32,48},{40,56},{48,32},{56,40},{64,80... | collective-permute-start | bytes 1179656 | tf_op jit(solution)/shard_map/ppermute | solution.py:30
  61.6 18.9 %collective-permute-start.6 = (f32[6,32,512]{2,1,0:T(8,128)}, f32[6,32,512]{2,1,0:T(8,128)}, u32[]{:S(2)}, u32[]{:S(2)}) collective-permute-start(f32[6,32,512]{2,1,0:T(8,128)} %get-tuple-element.79), channel_id=1, source_target_pairs={{0,8},{8,16},{16,24},{24,0},{32,40},{40,48},{48,56},{56,32},{64,72... | collective-permute-start | bytes 1179656 | tf_op jit(solution)/shard_map/ppermute | solution.py:30
  63.2 17.3 %collective-permute-start.8 = (f32[6,32,512]{2,1,0:T(8,128)}, f32[6,32,512]{2,1,0:T(8,128)}, u32[]{:S(2)}, u32[]{:S(2)}) collective-permute-start(f32[6,32,512]{2,1,0:T(8,128)} %get-tuple-element.80), channel_id=1, source_target_pairs={{0,24},{8,0},{16,8},{24,16},{32,56},{40,32},{48,40},{56,48},{64,88... | collective-permute-start | bytes 1179656 | tf_op jit(solution)/shard_map/ppermute | solution.py:30
  64.8 17.6 %collective-permute-start.9 = (f32[6,32,512]{2,1,0:T(8,128)}, f32[6,32,512]{2,1,0:T(8,128)}, u32[]{:S(2)}, u32[]{:S(2)}) collective-permute-start(f32[6,32,512]{2,1,0:T(8,128)} %get-tuple-element.72), channel_id=1, source_target_pairs={{0,96},{8,104},{16,112},{24,120},{32,0},{40,8},{48,16},{56,24},{64... | collective-permute-start | bytes 1179656 | tf_op jit(solution)/shard_map/ppermute | solution.py:30
  71.5 11.0 %collective-permute-start.11 = (f32[6,32,512]{2,1,0:T(8,128)}, f32[6,32,512]{2,1,0:T(8,128)}, u32[]{:S(2)}, u32[]{:S(2)}) collective-permute-start(f32[6,32,512]{2,1,0:T(8,128)} %get-tuple-element.41), channel_id=1, source_target_pairs={{0,64},{8,72},{16,80},{24,88},{32,96},{40,104},{48,112},{56,120},{... | collective-permute-start | bytes 1179656 | tf_op jit(solution)/shard_map/ppermute | solution.py:30
  85.7 93.9 %all-gather.10.cloned.1.call-start = ((), (), s32[]{:S(2)}) async-start(), calls=%async_computation.4 | async-start | bytes 3538944 | tf_op jit(solution)/shard_map/all_gather | solution.py:298
  85.8 28.2 %copy-start.3 = (s32[6]{0:T(128)}, s32[6]{0:T(128)S(1)}, u32[]{:S(2)}) copy-start(s32[6]{0:T(128)S(1)} %get-tuple-element.66.owner_ref) | copy-start | bytes 76
  90.8 39.8 %copy-start.2 = (f32[6,64,512]{2,1,0:T(8,128)S(1)}, f32[6,64,512]{2,1,0:T(8,128)}, u32[]{:S(2)}) copy-start(f32[6,64,512]{2,1,0:T(8,128)} %param.9) | copy-start | bytes 2359300
  121.5 33.8 %copy-start.4 = (s32[6]{0:T(128)S(1)}, s32[6]{0:T(128)}, u32[]{:S(2)}) copy-start(s32[6]{0:T(128)} %convert_reduce_fusion.rank_ref) | copy-start | bytes 76
  132.9 8.3 %collective-permute-start.13 = (bf16[6,32,512]{2,1,0:T(8,128)(2,1)S(1)}, bf16[6,32,512]{2,1,0:T(8,128)(2,1)S(1)}, u32[]{:S(2)}, u32[]{:S(2)}) collective-permute-start(bf16[6,32,512]{2,1,0:T(8,128)(2,1)S(1)} %get-tuple-element.52), channel_id=1, source_target_pairs={{0,32},{8,40},{16,48},{24,56},{32,64},{40,72},{48,80},{56,88},{64,... | collective-permute-start | bytes 589832 | tf_op jit(solution)/shard_map/ppermute | solution.py:30
  134.5 8.7 %collective-permute-start.12 = (bf16[6,32,512]{2,1,0:T(8,128)(2,1)S(1)}, bf16[6,32,512]{2,1,0:T(8,128)(2,1)S(1)}, u32[]{:S(2)}, u32[]{:S(2)}) collective-permute-start(bf16[6,32,512]{2,1,0:T(8,128)(2,1)S(1)} %get-tuple-element.92), channel_id=1, source_target_pairs={{0,8},{8,16},{16,24},{24,0},{32,40},{40,48},{48,56},{56,32},{64,72... | collective-permute-start | bytes 589832 | tf_op jit(solution)/shard_map/ppermute | solution.py:30
  136.0 9.5 %collective-permute-start.14 = (bf16[6,32,512]{2,1,0:T(8,128)(2,1)S(1)}, bf16[6,32,512]{2,1,0:T(8,128)(2,1)S(1)}, u32[]{:S(2)}, u32[]{:S(2)}) collective-permute-start(bf16[6,32,512]{2,1,0:T(8,128)(2,1)S(1)} %get-tuple-element.92), channel_id=1, source_target_pairs={{0,24},{8,0},{16,8},{24,16},{32,56},{40,32},{48,40},{56,48},{64,88... | collective-permute-start | bytes 589832 | tf_op jit(solution)/shard_map/ppermute | solution.py:30
  137.8 9.3 %collective-permute-start.15 = (bf16[6,32,512]{2,1,0:T(8,128)(2,1)S(1)}, bf16[6,32,512]{2,1,0:T(8,128)(2,1)S(1)}, u32[]{:S(2)}, u32[]{:S(2)}) collective-permute-start(bf16[6,32,512]{2,1,0:T(8,128)(2,1)S(1)} %get-tuple-element.52), channel_id=1, source_target_pairs={{0,96},{8,104},{16,112},{24,120},{32,0},{40,8},{48,16},{56,24},{64... | collective-permute-start | bytes 589832 | tf_op jit(solution)/shard_map/ppermute | solution.py:30
  139.5 7.8 %collective-permute-start.16 = (bf16[6,32,512]{2,1,0:T(8,128)(2,1)S(1)}, bf16[6,32,512]{2,1,0:T(8,128)(2,1)S(1)}, u32[]{:S(2)}, u32[]{:S(2)}) collective-permute-start(bf16[6,32,512]{2,1,0:T(8,128)(2,1)S(1)} %get-tuple-element.92), channel_id=1, source_target_pairs={{0,16},{8,24},{16,0},{24,8},{32,48},{40,56},{48,32},{56,40},{64,80... | collective-permute-start | bytes 589832 | tf_op jit(solution)/shard_map/ppermute | solution.py:30
  141.3 7.2 %collective-permute-start.17 = (bf16[6,32,512]{2,1,0:T(8,128)(2,1)S(1)}, bf16[6,32,512]{2,1,0:T(8,128)(2,1)S(1)}, u32[]{:S(2)}, u32[]{:S(2)}) collective-permute-start(bf16[6,32,512]{2,1,0:T(8,128)(2,1)S(1)} %get-tuple-element.52), channel_id=1, source_target_pairs={{0,64},{8,72},{16,80},{24,88},{32,96},{40,104},{48,112},{56,120},{... | collective-permute-start | bytes 589832 | tf_op jit(solution)/shard_map/ppermute | solution.py:30
  148.5 18.3 %collective-permute-start.22 = (bf16[4,6,32,512]{3,2,1,0:T(8,128)(2,1)S(1)}, bf16[4,6,32,512]{3,2,1,0:T(8,128)(2,1)S(1)}, u32[]{:S(2)}, u32[]{:S(2)}) collective-permute-start(bf16[4,6,32,512]{3,2,1,0:T(8,128)(2,1)S(1)} %pad_maximum_fusion.2.refs_1_), channel_id=1, source_target_pairs={{0,8},{8,16},{16,24},{24,0},{32,40},{40,48},{48,56},{56,32},{64,72... | collective-permute-start | bytes 2359304 | tf_op jit(solution)/shard_map/ppermute | solution.py:30
  149.6 17.6 %collective-permute-start.24 = (bf16[4,6,32,512]{3,2,1,0:T(8,128)(2,1)S(1)}, bf16[4,6,32,512]{3,2,1,0:T(8,128)(2,1)S(1)}, u32[]{:S(2)}, u32[]{:S(2)}) collective-permute-start(bf16[4,6,32,512]{3,2,1,0:T(8,128)(2,1)S(1)} %pad_maximum_fusion.2.refs_1_), channel_id=1, source_target_pairs={{0,24},{8,0},{16,8},{24,16},{32,56},{40,32},{48,40},{56,48},{64,88... | collective-permute-start | bytes 2359304 | tf_op jit(solution)/shard_map/ppermute | solution.py:30
  152.0 19.2 %collective-permute-start.18 = (bf16[4,6,32,512]{3,2,1,0:T(8,128)(2,1)S(1)}, bf16[4,6,32,512]{3,2,1,0:T(8,128)(2,1)S(1)}, u32[]{:S(2)}, u32[]{:S(2)}) collective-permute-start(bf16[4,6,32,512]{3,2,1,0:T(8,128)(2,1)S(1)} %pad_maximum_fusion.1.refs_0_), channel_id=1, source_target_pairs={{0,32},{8,40},{16,48},{24,56},{32,64},{40,72},{48,80},{56,88},{64,... | collective-permute-start | bytes 2359304 | tf_op jit(solution)/shard_map/ppermute | solution.py:30
  153.6 20.8 %collective-permute-start.20 = (bf16[4,6,32,512]{3,2,1,0:T(8,128)(2,1)S(1)}, bf16[4,6,32,512]{3,2,1,0:T(8,128)(2,1)S(1)}, u32[]{:S(2)}, u32[]{:S(2)}) collective-permute-start(bf16[4,6,32,512]{3,2,1,0:T(8,128)(2,1)S(1)} %pad_maximum_fusion.1.refs_0_), channel_id=1, source_target_pairs={{0,96},{8,104},{16,112},{24,120},{32,0},{40,8},{48,16},{56,24},{64... | collective-permute-start | bytes 2359304 | tf_op jit(solution)/shard_map/ppermute | solution.py:30
  166.9 20.4 %collective-permute-start.23 = (bf16[2,6,32,512]{3,2,1,0:T(8,128)(2,1)S(1)}, bf16[2,6,32,512]{3,2,1,0:T(8,128)(2,1)S(1)}, u32[]{:S(2)}, u32[]{:S(2)}) collective-permute-start(bf16[2,6,32,512]{3,2,1,0:T(8,128)(2,1)S(1)} %slice.41), channel_id=1, source_target_pairs={{0,8},{8,16},{16,24},{24,0},{32,40},{40,48},{48,56},{56,32},{64,72... | collective-permute-start | bytes 1179656 | tf_op jit(solution)/shard_map/ppermute | solution.py:30
  168.0 19.3 %collective-permute-start.25 = (bf16[2,6,32,512]{3,2,1,0:T(8,128)(2,1)}, bf16[2,6,32,512]{3,2,1,0:T(8,128)(2,1)S(1)}, u32[]{:S(2)}, u32[]{:S(2)}) collective-permute-start(bf16[2,6,32,512]{3,2,1,0:T(8,128)(2,1)} %slice.42), channel_id=1, source_target_pairs={{0,24},{8,0},{16,8},{24,16},{32,56},{40,32},{48,40},{56,48},{64,88... | collective-permute-start | bytes 1179656 | tf_op jit(solution)/shard_map/ppermute | solution.py:30
  172.0 15.4 %collective-permute-start.19 = (bf16[2,6,32,512]{3,2,1,0:T(8,128)(2,1)}, bf16[2,6,32,512]{3,2,1,0:T(8,128)(2,1)S(1)}, u32[]{:S(2)}, u32[]{:S(2)}) collective-permute-start(bf16[2,6,32,512]{3,2,1,0:T(8,128)(2,1)} %slice.39), channel_id=1, source_target_pairs={{0,32},{8,40},{16,48},{24,56},{32,64},{40,72},{48,80},{56,88},{64,... | collective-permute-start | bytes 1179656 | tf_op jit(solution)/shard_map/ppermute | solution.py:30
  175.2 12.2 %collective-permute-start.21 = (bf16[2,6,32,512]{3,2,1,0:T(8,128)(2,1)}, bf16[2,6,32,512]{3,2,1,0:T(8,128)(2,1)S(1)}, u32[]{:S(2)}, u32[]{:S(2)}) collective-permute-start(bf16[2,6,32,512]{3,2,1,0:T(8,128)(2,1)} %slice.40), channel_id=1, source_target_pairs={{0,96},{8,104},{16,112},{24,120},{32,0},{40,8},{48,16},{56,24},{64... | collective-permute-start | bytes 1179656 | tf_op jit(solution)/shard_map/ppermute | solution.py:30
Sparse Core Ops, SparseCore 0:
  9.7 63.3 all-gather.7
  85.8 28.2 all-gather.5
  130.6 27.1 all-gather.9

commit v3 on v2

--- a/solution.py
+++ b/solution.py
@@ -167,7 +167,7 @@
             jax.ShapeDtypeStruct((blocks, slab_rows, width), jnp.float32),
             jax.ShapeDtypeStruct((8, 128), jnp.float32),
         ],
-        compiler_params=pltpu.CompilerParams(vmem_limit_bytes=VMEM),
+        compiler_params=pltpu.CompilerParams(vmem_limit_bytes=56 * 2**20),
         cost_estimate=pl.CostEstimate(
             flops=flops, bytes_accessed=blocks * width * width * 4, transcendentals=0
         ),

time: 196 us -> 196 us (level)
  transfers between devices with their start and end apart: 30 -> 30, of which waited for: 13 -> 13; matrix products, arithmetic and copies ran while one was open for 11% -> 11% of each run, Pallas kernels for 6% -> 5%
where the time goes in v3:
time: 196 us; the launch traced here: 194 us
  waiting for transfers between devices  80.9 us (41%)
  starting transfers between devices  46.5 us (24%)
  Pallas kernels  19.1 us (10%)
  between operations  14.1 us (7%)
  other arithmetic  13.4 us (7%)
  local copies, waits for them, and re-layouts  12.2 us (6%)
  blocking collectives  8.27 us (4%)
    ppermute x26, waiting for transfers between devices, send(): return lax.ppermute(value, 'dp', shift_perm(axis, step))  56.9 us
    ppermute x26, starting transfers between devices, send(): return lax.ppermute(value, 'dp', shift_perm(axis, step))  42.1 us
    all_gather x1, waiting for transfers between devices, shards(): high_whole = lax.all_gather(high, 'opt', axis=0)  23.3 us
    all_to_all x1, blocking collectives, shards(): lax.all_to_all(squares, 'opt', split_axis=0, concat_axis=0, tiled=True)  8.27 us
    pallas_call x1, Pallas kernels, directions(): pl.pallas_call(direction_kernel, grid_spec=grid_spec, out_shape=[jax.Shap...  7.39 us
    pallas_call x4, Pallas kernels, put(): pl.pallas_call(kernel, grid=(1,), out_shape=jax.ShapeDtypeStruct(shape, j...  7 us
    reshape x2, local copies, waits for them, and re-layouts, raw(): return got.reshape((SIDE, blocks, half_rows, width))  6.19 us
    pallas_call x1, Pallas kernels, factors(): pl.pallas_call(gram_kernel, grid_spec=grid_spec, out_shape=[jax.ShapeDtyp...  4.71 us
  transfers between devices with their start and end apart: 30, of which 13 were waited for; matrix products, arithmetic and copies ran while one was open for 11% of the time, Pallas kernels for 5%

profile of v3, /device:TPU:0, one launch (start us, length us, event | category | flops | bytes accessed | tf_op | source)
XLA Modules:
  0.0 194.4 jit_solution(15054962896611351176)
XLA Ops:
  8.0 3.1 %dynamic-slice_bitcast_fusion = (bf16[4,6,32,512]{3,2,1,0:T(8,128)(2,1)}, bf16[4,6,32,512]{3,2,1,0:T(8,128)(2,1)}, bf16[4,6,32,512]{3,2,1,0:T(8,128)(2,1)}) fusion(bf16[4,4,6,64,512]{4,3,2,1,0:T(8,128)(2,1)} %bitcast.102, s32[]{:T(128)S(6)} %select_n.146, s32[]{:T(128)S(6)} %select_n.142, s32[]{:T(128)S(6)} %select_n.138), kind=kLoop, calls=%fused_computation.11 | loop fusion | bytes 4718604 | tf_op jit(solution)/shard_map/reshape | solution.py:62
  11.1 2.0 %collective-permute-start.1 = (bf16[4,6,32,512]{3,2,1,0:T(8,128)(2,1)}, bf16[4,6,32,512]{3,2,1,0:T(8,128)(2,1)S(1)}, u32[]{:S(2)}, u32[]{:S(2)}) collective-permute-start(bf16[4,6,32,512]{3,2,1,0:T(8,128)(2,1)} %get-tuple-element.84), channel_id=1, source_target_pairs={{0,32},{8,40},{16,48},{24,56},{32,64},{40,72},{48,80},{56,88},{64,... | collective-permute-start | bytes 2359304 | tf_op jit(solution)/shard_map/ppermute | solution.py:30
  13.1 2.1 %collective-permute-start.3 = (bf16[4,6,32,512]{3,2,1,0:T(8,128)(2,1)}, bf16[4,6,32,512]{3,2,1,0:T(8,128)(2,1)S(1)}, u32[]{:S(2)}, u32[]{:S(2)}) collective-permute-start(bf16[4,6,32,512]{3,2,1,0:T(8,128)(2,1)} %get-tuple-element.83), channel_id=1, source_target_pairs={{0,96},{8,104},{16,112},{24,120},{32,0},{40,8},{48,16},{56,24},{64... | collective-permute-start | bytes 2359304 | tf_op jit(solution)/shard_map/ppermute | solution.py:30
  15.2 3.1 %dynamic-slice_bitcast_fusion.1 = (bf16[4,6,32,512]{3,2,1,0:T(8,128)(2,1)}, bf16[4,6,32,512]{3,2,1,0:T(8,128)(2,1)}, bf16[4,6,32,512]{3,2,1,0:T(8,128)(2,1)}) fusion(bf16[4,4,6,64,512]{4,3,2,1,0:T(8,128)(2,1)} %bitcast.103, s32[]{:T(128)S(6)} %select_n.144, s32[]{:T(128)S(6)} %select_n.140, s32[]{:T(128)S(6)} %select_n.136), kind=kLoop, calls=%fused_computation.12 | loop fusion | bytes 4718604 | tf_op jit(solution)/shard_map/reshape | solution.py:62
  18.3 1.6 collective-permute-start
  19.9 1.7 collective-permute-start.2
  21.5 2.0 %collective-permute-start.4 = (bf16[4,6,32,512]{3,2,1,0:T(8,128)(2,1)}, bf16[4,6,32,512]{3,2,1,0:T(8,128)(2,1)}, u32[]{:S(2)}, u32[]{:S(2)}) collective-permute-start(bf16[4,6,32,512]{3,2,1,0:T(8,128)(2,1)} %get-tuple-element.85), channel_id=1, source_target_pairs={{0,16},{8,24},{16,0},{24,8},{32,48},{40,56},{48,32},{56,40},{64,80... | collective-permute-start | bytes 2359304 | tf_op jit(solution)/shard_map/ppermute | solution.py:30
  23.5 9.4 %collective-permute-done.1 = bf16[4,6,32,512]{3,2,1,0:T(8,128)(2,1)S(1)} collective-permute-done((bf16[4,6,32,512]{3,2,1,0:T(8,128)(2,1)}, bf16[4,6,32,512]{3,2,1,0:T(8,128)(2,1)S(1)}, u32[]{:S(2)}, u32[]{:S(2)}) %collective-permute-start.1) | collective-permute-done | bytes 786464 | tf_op jit(solution)/shard_map/ppermute | solution.py:30
  33.0 1.6 collective-permute-start.5
  34.5 1.1 copy.22
  35.6 4.3 %all-to-all-start = ((bf16[2,8,64,512]{3,2,0,1:T(8,128)(2,1)}), bf16[2,8,64,512]{3,2,0,1:T(8,128)(2,1)S(1)}, u32[]{:S(2)}, u32[]{:S(2)}) async-start(bf16[2,8,64,512]{3,2,0,1:T(8,128)(2,1)} %copy.22), calls=%async_computation | async-start | bytes 2097152 | tf_op jit(solution)/shard_map/all_to_all | solution.py:271
  40.7 16.2 %collective-permute-done.4 = bf16[4,6,32,512]{3,2,1,0:T(8,128)(2,1)} collective-permute-done((bf16[4,6,32,512]{3,2,1,0:T(8,128)(2,1)}, bf16[4,6,32,512]{3,2,1,0:T(8,128)(2,1)}, u32[]{:S(2)}, u32[]{:S(2)}) %collective-permute-start.4) | collective-permute-done | bytes 786464 | tf_op jit(solution)/shard_map/ppermute | solution.py:30
  56.9 3.5 %fusion.6 = (f32[6,32,512]{2,1,0:T(8,128)}, f32[6,32,512]{2,1,0:T(8,128)}, f32[6,32,512]{2,1,0:T(8,128)S(1)}, f32[6,32,512]{2,1,0:T(8,128)}, f32[6,32,512]{2,1,0:T(8,128)}, /*index=5*/f32[6,32,512]{2,1,0:T(8,128)}) fusion(bf16[4,6,32,512]{3,2,1,0:T(8,128)(2,1)} %collective-permute-done.4, s32[]{:T(128)S(6)} %select_n.146, ...), kind=kLoop, calls=%fused_computation.22 | loop fusion | flops 4128768 | bytes 7077920 | tf_op jit(solution)/shard_map/add | solution.py:73
  60.5 1.1 collective-permute-start.10
  61.6 1.6 collective-permute-start.6
  63.2 1.6 collective-permute-start.8
  64.8 3.2 %collective-permute-start.9 = (f32[6,32,512]{2,1,0:T(8,128)}, f32[6,32,512]{2,1,0:T(8,128)}, u32[]{:S(2)}, u32[]{:S(2)}) collective-permute-start(f32[6,32,512]{2,1,0:T(8,128)} %get-tuple-element.72), channel_id=1, source_target_pairs={{0,96},{8,104},{16,112},{24,120},{32,0},{40,8},{48,16},{56,24},{64... | collective-permute-start | bytes 1179656 | tf_op jit(solution)/shard_map/ppermute | solution.py:30
  68.0 3.5 %collective-permute-done.7 = f32[6,32,512]{2,1,0:T(8,128)} collective-permute-done((f32[6,32,512]{2,1,0:T(8,128)S(1)}, f32[6,32,512]{2,1,0:T(8,128)}, u32[]{:S(2)}, u32[]{:S(2)}) %collective-permute-start.7) | collective-permute-done | bytes 393248 | tf_op jit(solution)/shard_map/ppermute | solution.py:30
  71.5 2.9 %collective-permute-done.10 = f32[6,32,512]{2,1,0:T(8,128)} collective-permute-done((f32[6,32,512]{2,1,0:T(8,128)}, f32[6,32,512]{2,1,0:T(8,128)}, u32[]{:S(2)}, u32[]{:S(2)}) %collective-permute-start.10) | collective-permute-done | bytes 393248 | tf_op jit(solution)/shard_map/ppermute | solution.py:30
  74.4 6.1 %collective-permute-done.6 = f32[6,32,512]{2,1,0:T(8,128)} collective-permute-done((f32[6,32,512]{2,1,0:T(8,128)}, f32[6,32,512]{2,1,0:T(8,128)}, u32[]{:S(2)}, u32[]{:S(2)}) %collective-permute-start.6) | collective-permute-done | bytes 393248 | tf_op jit(solution)/shard_map/ppermute | solution.py:30
  80.5 1.9 collective-permute-done.9
  82.4 2.4 %fusion.14 = (f32[6,32,512]{2,1,0:T(8,128)S(1)}, f32[6,32,512]{2,1,0:T(8,128)S(1)}) fusion(f32[6,32,512]{2,1,0:T(8,128)} %collective-permute-done.7, f32[6,32,512]{2,1,0:T(8,128)} %collective-permute-done.9, f32[6,32,512]{2,1,0:T(8,128)} %collective-permute-done.11, bf16[4,6,32,512]{3,2,1,0:T(8,128)(2,1)} %collective-permute-done.4, s32[]{:T(128)S(6)} %select_n.132, ...), kind=kLoop, calls=%fused_computation.36 | loop fusion | flops 1966080 | bytes 4718608 | tf_op jit(solution)/shard_map/add | solution.py:79
  87.6 2.5 %multiply_reduce_fusion = (f32[6]{0:T(128)S(1)}, f32[6,64,512]{2,1,0:T(8,128)}, bf16[6,64,512]{2,1,0:T(8,128)(2,1)}) fusion(f32[6,32,512]{2,1,0:T(8,128)S(1)} %get-tuple-element.78, f32[6,32,512]{2,1,0:T(8,128)S(1)} %get-tuple-element.77, f32[6,64,512]{2,1,0:T(8,128)} %param.10), kind=kLoop, calls=%fused_computation.10 | loop fusion | flops 2359290 | bytes 2752536 | tf_op jit(solution)/shard_map/reduce_sum | solution.py:287
  90.8 23.3 %all-gather.6.cloned.1.call-done.grad_ref.high_ref = bf16[8,6,64,512]{3,2,1,0:T(8,128)(2,1)} async-done(((bf16[1,6,64,512]{3,2,1,0:T(8,128)(2,1)}), bf16[8,6,64,512]{3,2,1,0:T(8,128)(2,1)}) %all-gather.6.cloned.1.call-update) | async-done | bytes 3145744 | tf_op jit(solution)/shard_map/all_gather | solution.py:284
  114.1 7.4 %directions.1 = (f32[6,64,512]{2,1,0:T(8,128)}, f32[8,128]{1,0:T(8,128)}) custom-call(s32[6]{0:T(128)} %copy-done.3, s32[6]{0:T(128)} %convert_reduce_fusion.rank_ref, bf16[2,8,64,512]{3,2,1,0:T(8,128)(2,1)} %copy.23.left_ref, bf16[8,6,64,512]{3,2,1,0:T(8,128)(2,1)} %all-gather.6.cloned.1.call-done.grad_ref.high_ref, bf16[8,2,512,512]{3,2,1,0:T(8,128)(2,1)} %bitcast.101, ...), custom_call_target="tpu_custom_call" | custom-call | flops 402653184 | bytes 6291456 | tf_op jit(solution)/shard_map/directions/pallas_call | solution.py:163
  122.2 8.3 %all_to_all.10 = f32[8,8,128]{2,1,0:T(8,128)S(1)} all-to-all(f32[8,8,128]{2,1,0:T(8,128)S(1)} %broadcast_in_dim.17), channel_id=1, replica_groups=mesh['dp'=16,'opt'=8] {'opt'}, dimensions={0} | all-to-all | bytes 65536 | tf_op jit(solution)/shard_map/all_to_all | solution.py:291
  130.6 2.3 %fusion.19 = (bf16[6,64,512]{2,1,0:T(8,128)(2,1)S(1)}, f32[6,64,512]{2,1,0:T(8,128)}) fusion(f32[6,64,512]{2,1,0:T(8,128)S(1)} %copy-done.2, f32[6,64,512]{2,1,0:T(8,128)} %get-tuple-element.51, f32[6]{0:T(128)S(1)} %fusion.17), kind=kLoop, calls=%fused_computation.51 | loop fusion | flops 589824 | bytes 2752536 | tf_op jit(solution)/shard_map/convert_element_type | solution.py:300
  132.9 1.6 collective-permute-start.13
  134.5 1.5 collective-permute-start.12
  136.0 1.8 collective-permute-start.14
  137.8 1.7 collective-permute-start.15
  139.5 1.8 collective-permute-start.16
  141.3 1.9 collective-permute-start.17
  143.2 2.4 %collective-permute-done.14 = bf16[6,32,512]{2,1,0:T(8,128)(2,1)S(1)} collective-permute-done((bf16[6,32,512]{2,1,0:T(8,128)(2,1)S(1)}, bf16[6,32,512]{2,1,0:T(8,128)(2,1)S(1)}, u32[]{:S(2)}, u32[]{:S(2)}) %collective-permute-start.14) | collective-permute-done | bytes 196640 | tf_op jit(solution)/shard_map/ppermute | solution.py:30
  145.6 1.5 collective-permute-done.15
  147.2 1.2 collective-permute-done.17
  148.5 1.1 collective-permute-start.22
  149.6 2.2 %collective-permute-start.24 = (bf16[4,6,32,512]{3,2,1,0:T(8,128)(2,1)S(1)}, bf16[4,6,32,512]{3,2,1,0:T(8,128)(2,1)S(1)}, u32[]{:S(2)}, u32[]{:S(2)}) collective-permute-start(bf16[4,6,32,512]{3,2,1,0:T(8,128)(2,1)S(1)} %pad_maximum_fusion.2.refs_1_), channel_id=1, source_target_pairs={{0,24},{8,0},{16,8},{24,16},{32,56},{40,32},{48,40},{56,48},{64,88... | collective-permute-start | bytes 2359304 | tf_op jit(solution)/shard_map/ppermute | solution.py:30
  152.0 1.6 collective-permute-start.18
  153.6 1.7 collective-permute-start.20
  155.9 10.9 %collective-permute-done.22.refs_1_ = bf16[4,6,32,512]{3,2,1,0:T(8,128)(2,1)S(1)} collective-permute-done((bf16[4,6,32,512]{3,2,1,0:T(8,128)(2,1)S(1)}, bf16[4,6,32,512]{3,2,1,0:T(8,128)(2,1)S(1)}, u32[]{:S(2)}, u32[]{:S(2)}) %collective-permute-start.22) | collective-permute-done | bytes 786464 | tf_op jit(solution)/shard_map/ppermute | solution.py:30
  168.0 3.2 %collective-permute-start.25 = (bf16[2,6,32,512]{3,2,1,0:T(8,128)(2,1)}, bf16[2,6,32,512]{3,2,1,0:T(8,128)(2,1)S(1)}, u32[]{:S(2)}, u32[]{:S(2)}) collective-permute-start(bf16[2,6,32,512]{3,2,1,0:T(8,128)(2,1)} %slice.42), channel_id=1, source_target_pairs={{0,24},{8,0},{16,8},{24,16},{32,56},{40,32},{48,40},{56,48},{64,88... | collective-permute-start | bytes 1179656 | tf_op jit(solution)/shard_map/ppermute | solution.py:30
  172.0 2.4 %collective-permute-start.19 = (bf16[2,6,32,512]{3,2,1,0:T(8,128)(2,1)}, bf16[2,6,32,512]{3,2,1,0:T(8,128)(2,1)S(1)}, u32[]{:S(2)}, u32[]{:S(2)}) collective-permute-start(bf16[2,6,32,512]{3,2,1,0:T(8,128)(2,1)} %slice.39), channel_id=1, source_target_pairs={{0,32},{8,40},{16,48},{24,56},{32,64},{40,72},{48,80},{56,88},{64,... | collective-permute-start | bytes 1179656 | tf_op jit(solution)/shard_map/ppermute | solution.py:30
  176.1 1.7 place_weights.4.refs_2_
  177.8 1.8 place_weights.5.refs_2_
  179.6 4.7 %factors.1 = (f32[1,1,2,512,512]{4,3,2,1,0:T(8,128)}, f32[1,1,2,512,512]{4,3,2,1,0:T(8,128)}) custom-call(s32[2]{0:T(128)} %get-tuple-element.64.block_ref, s32[2]{0:T(128)} %get-tuple-element.63.used_ref, bf16[8,6,64,512]{3,2,1,0:T(8,128)(2,1)} %all-gather.6.cloned.1.call-done.grad_ref.high_ref, bf16[8,6,64,512]{3,2,1,0:T(8,128)(2,1)} %bitcast.117, ...), custom_call_target="tpu_custom_call" | custom-call | flops 3221225472 | bytes 10485760 | tf_op jit(solution)/shard_map/factors/pallas_call | solution.py:215
  184.3 1.7 place_weights.6.refs_4_
  186.1 1.8 place_weights.7
  (59 shorter events, 10.4 us)
Async XLA Ops:
  7.2 27.4 %copy-start = (bf16[1,1,2,512,512]{4,3,2,1,0:T(8,128)(2,1)S(1)}, bf16[1,1,2,512,512]{4,3,2,1,0:T(8,128)(2,1)}, u32[]{:S(2)}) copy-start(bf16[1,1,2,512,512]{4,3,2,1,0:T(8,128)(2,1)} %param.14) | copy-start | bytes 3145732
  7.2 75.3 %all-gather.8.cloned.1.call-start = ((), (), s32[]{:S(2)}) async-start(), calls=%async_computation.3 | async-start | bytes 9437184 | tf_op jit(solution)/shard_map/all_gather | solution.py:270
  11.1 21.9 %collective-permute-start.1 = (bf16[4,6,32,512]{3,2,1,0:T(8,128)(2,1)}, bf16[4,6,32,512]{3,2,1,0:T(8,128)(2,1)S(1)}, u32[]{:S(2)}, u32[]{:S(2)}) collective-permute-start(bf16[4,6,32,512]{3,2,1,0:T(8,128)(2,1)} %get-tuple-element.84), channel_id=1, source_target_pairs={{0,32},{8,40},{16,48},{24,56},{32,64},{40,72},{48,80},{56,88},{64,... | collective-permute-start | bytes 2359304 | tf_op jit(solution)/shard_map/ppermute | solution.py:30
  13.1 26.9 %collective-permute-start.3 = (bf16[4,6,32,512]{3,2,1,0:T(8,128)(2,1)}, bf16[4,6,32,512]{3,2,1,0:T(8,128)(2,1)S(1)}, u32[]{:S(2)}, u32[]{:S(2)}) collective-permute-start(bf16[4,6,32,512]{3,2,1,0:T(8,128)(2,1)} %get-tuple-element.83), channel_id=1, source_target_pairs={{0,96},{8,104},{16,112},{24,120},{32,0},{40,8},{48,16},{56,24},{64... | collective-permute-start | bytes 2359304 | tf_op jit(solution)/shard_map/ppermute | solution.py:30
  18.3 21.7 %collective-permute-start = (bf16[4,6,32,512]{3,2,1,0:T(8,128)(2,1)}, bf16[4,6,32,512]{3,2,1,0:T(8,128)(2,1)S(1)}, u32[]{:S(2)}, u32[]{:S(2)}) collective-permute-start(bf16[4,6,32,512]{3,2,1,0:T(8,128)(2,1)} %get-tuple-element.87), channel_id=1, source_target_pairs={{0,8},{8,16},{16,24},{24,0},{32,40},{40,48},{48,56},{56,32},{64,72... | collective-permute-start | bytes 2359304 | tf_op jit(solution)/shard_map/ppermute | solution.py:30
  19.9 20.8 %collective-permute-start.2 = (bf16[4,6,32,512]{3,2,1,0:T(8,128)(2,1)}, bf16[4,6,32,512]{3,2,1,0:T(8,128)(2,1)}, u32[]{:S(2)}, u32[]{:S(2)}) collective-permute-start(bf16[4,6,32,512]{3,2,1,0:T(8,128)(2,1)} %get-tuple-element.86), channel_id=1, source_target_pairs={{0,24},{8,0},{16,8},{24,16},{32,56},{40,32},{48,40},{56,48},{64,88... | collective-permute-start | bytes 2359304 | tf_op jit(solution)/shard_map/ppermute | solution.py:30
  21.5 35.4 %collective-permute-start.4 = (bf16[4,6,32,512]{3,2,1,0:T(8,128)(2,1)}, bf16[4,6,32,512]{3,2,1,0:T(8,128)(2,1)}, u32[]{:S(2)}, u32[]{:S(2)}) collective-permute-start(bf16[4,6,32,512]{3,2,1,0:T(8,128)(2,1)} %get-tuple-element.85), channel_id=1, source_target_pairs={{0,16},{8,24},{16,0},{24,8},{32,48},{40,56},{48,32},{56,40},{64,80... | collective-permute-start | bytes 2359304 | tf_op jit(solution)/shard_map/ppermute | solution.py:30
  33.0 24.0 %collective-permute-start.5 = (bf16[4,6,32,512]{3,2,1,0:T(8,128)(2,1)}, bf16[4,6,32,512]{3,2,1,0:T(8,128)(2,1)}, u32[]{:S(2)}, u32[]{:S(2)}) collective-permute-start(bf16[4,6,32,512]{3,2,1,0:T(8,128)(2,1)} %get-tuple-element.34), channel_id=1, source_target_pairs={{0,64},{8,72},{16,80},{24,88},{32,96},{40,104},{48,112},{56,120},{... | collective-permute-start | bytes 2359304 | tf_op jit(solution)/shard_map/ppermute | solution.py:30
  35.6 46.8 %all-to-all-start = ((bf16[2,8,64,512]{3,2,0,1:T(8,128)(2,1)}), bf16[2,8,64,512]{3,2,0,1:T(8,128)(2,1)S(1)}, u32[]{:S(2)}, u32[]{:S(2)}) async-start(bf16[2,8,64,512]{3,2,0,1:T(8,128)(2,1)} %copy.22), calls=%async_computation | async-start | bytes 2097152 | tf_op jit(solution)/shard_map/all_to_all | solution.py:271
  39.9 74.2 %all-gather.6.cloned.1.call-start = ((), (), s32[]{:S(2)}) async-start(), calls=%async_computation.2 | async-start | bytes 3538944 | tf_op jit(solution)/shard_map/all_gather | solution.py:284
  40.0 45.8 %copy-start.5 = (s32[96,1]{0,1:T(1,128)S(1)}, s32[96,1]{0,1:T(1,128)}, u32[]{:S(2)}) copy-start(s32[96,1]{0,1:T(1,128)} %param.11) | copy-start | bytes 1156
  40.0 42.4 %copy-start.1 = (bf16[4,6,32,512]{3,2,1,0:T(8,128)(2,1)}, bf16[4,6,32,512]{3,2,1,0:T(8,128)(2,1)S(1)}, u32[]{:S(2)}) copy-start(bf16[4,6,32,512]{3,2,1,0:T(8,128)(2,1)S(1)} %collective-permute-done) | copy-start | bytes 2359300
  60.5 11.0 %collective-permute-start.7 = (f32[6,32,512]{2,1,0:T(8,128)S(1)}, f32[6,32,512]{2,1,0:T(8,128)}, u32[]{:S(2)}, u32[]{:S(2)}) collective-permute-start(f32[6,32,512]{2,1,0:T(8,128)S(1)} %get-tuple-element.73), channel_id=1, source_target_pairs={{0,32},{8,40},{16,48},{24,56},{32,64},{40,72},{48,80},{56,88},{64,... | collective-permute-start | bytes 1179656 | tf_op jit(solution)/shard_map/ppermute | solution.py:30
  60.5 14.0 %collective-permute-start.10 = (f32[6,32,512]{2,1,0:T(8,128)}, f32[6,32,512]{2,1,0:T(8,128)}, u32[]{:S(2)}, u32[]{:S(2)}) collective-permute-start(f32[6,32,512]{2,1,0:T(8,128)} %get-tuple-element.81), channel_id=1, source_target_pairs={{0,16},{8,24},{16,0},{24,8},{32,48},{40,56},{48,32},{56,40},{64,80... | collective-permute-start | bytes 1179656 | tf_op jit(solution)/shard_map/ppermute | solution.py:30
  61.6 18.9 %collective-permute-start.6 = (f32[6,32,512]{2,1,0:T(8,128)}, f32[6,32,512]{2,1,0:T(8,128)}, u32[]{:S(2)}, u32[]{:S(2)}) collective-permute-start(f32[6,32,512]{2,1,0:T(8,128)} %get-tuple-element.79), channel_id=1, source_target_pairs={{0,8},{8,16},{16,24},{24,0},{32,40},{40,48},{48,56},{56,32},{64,72... | collective-permute-start | bytes 1179656 | tf_op jit(solution)/shard_map/ppermute | solution.py:30
  63.2 17.3 %collective-permute-start.8 = (f32[6,32,512]{2,1,0:T(8,128)}, f32[6,32,512]{2,1,0:T(8,128)}, u32[]{:S(2)}, u32[]{:S(2)}) collective-permute-start(f32[6,32,512]{2,1,0:T(8,128)} %get-tuple-element.80), channel_id=1, source_target_pairs={{0,24},{8,0},{16,8},{24,16},{32,56},{40,32},{48,40},{56,48},{64,88... | collective-permute-start | bytes 1179656 | tf_op jit(solution)/shard_map/ppermute | solution.py:30
  64.8 17.6 %collective-permute-start.9 = (f32[6,32,512]{2,1,0:T(8,128)}, f32[6,32,512]{2,1,0:T(8,128)}, u32[]{:S(2)}, u32[]{:S(2)}) collective-permute-start(f32[6,32,512]{2,1,0:T(8,128)} %get-tuple-element.72), channel_id=1, source_target_pairs={{0,96},{8,104},{16,112},{24,120},{32,0},{40,8},{48,16},{56,24},{64... | collective-permute-start | bytes 1179656 | tf_op jit(solution)/shard_map/ppermute | solution.py:30
  71.5 11.0 %collective-permute-start.11 = (f32[6,32,512]{2,1,0:T(8,128)}, f32[6,32,512]{2,1,0:T(8,128)}, u32[]{:S(2)}, u32[]{:S(2)}) collective-permute-start(f32[6,32,512]{2,1,0:T(8,128)} %get-tuple-element.41), channel_id=1, source_target_pairs={{0,64},{8,72},{16,80},{24,88},{32,96},{40,104},{48,112},{56,120},{... | collective-permute-start | bytes 1179656 | tf_op jit(solution)/shard_map/ppermute | solution.py:30
  85.7 93.9 %all-gather.10.cloned.1.call-start = ((), (), s32[]{:S(2)}) async-start(), calls=%async_computation.4 | async-start | bytes 3538944 | tf_op jit(solution)/shard_map/all_gather | solution.py:298
  85.8 28.2 %copy-start.3 = (s32[6]{0:T(128)}, s32[6]{0:T(128)S(1)}, u32[]{:S(2)}) copy-start(s32[6]{0:T(128)S(1)} %get-tuple-element.66.owner_ref) | copy-start | bytes 76
  90.8 39.8 %copy-start.2 = (f32[6,64,512]{2,1,0:T(8,128)S(1)}, f32[6,64,512]{2,1,0:T(8,128)}, u32[]{:S(2)}) copy-start(f32[6,64,512]{2,1,0:T(8,128)} %param.9) | copy-start | bytes 2359300
  121.5 33.8 %copy-start.4 = (s32[6]{0:T(128)S(1)}, s32[6]{0:T(128)}, u32[]{:S(2)}) copy-start(s32[6]{0:T(128)} %convert_reduce_fusion.rank_ref) | copy-start | bytes 76
  132.9 8.3 %collective-permute-start.13 = (bf16[6,32,512]{2,1,0:T(8,128)(2,1)S(1)}, bf16[6,32,512]{2,1,0:T(8,128)(2,1)S(1)}, u32[]{:S(2)}, u32[]{:S(2)}) collective-permute-start(bf16[6,32,512]{2,1,0:T(8,128)(2,1)S(1)} %get-tuple-element.52), channel_id=1, source_target_pairs={{0,32},{8,40},{16,48},{24,56},{32,64},{40,72},{48,80},{56,88},{64,... | collective-permute-start | bytes 589832 | tf_op jit(solution)/shard_map/ppermute | solution.py:30
  134.5 8.7 %collective-permute-start.12 = (bf16[6,32,512]{2,1,0:T(8,128)(2,1)S(1)}, bf16[6,32,512]{2,1,0:T(8,128)(2,1)S(1)}, u32[]{:S(2)}, u32[]{:S(2)}) collective-permute-start(bf16[6,32,512]{2,1,0:T(8,128)(2,1)S(1)} %get-tuple-element.92), channel_id=1, source_target_pairs={{0,8},{8,16},{16,24},{24,0},{32,40},{40,48},{48,56},{56,32},{64,72... | collective-permute-start | bytes 589832 | tf_op jit(solution)/shard_map/ppermute | solution.py:30
  136.0 9.5 %collective-permute-start.14 = (bf16[6,32,512]{2,1,0:T(8,128)(2,1)S(1)}, bf16[6,32,512]{2,1,0:T(8,128)(2,1)S(1)}, u32[]{:S(2)}, u32[]{:S(2)}) collective-permute-start(bf16[6,32,512]{2,1,0:T(8,128)(2,1)S(1)} %get-tuple-element.92), channel_id=1, source_target_pairs={{0,24},{8,0},{16,8},{24,16},{32,56},{40,32},{48,40},{56,48},{64,88... | collective-permute-start | bytes 589832 | tf_op jit(solution)/shard_map/ppermute | solution.py:30
  137.8 9.3 %collective-permute-start.15 = (bf16[6,32,512]{2,1,0:T(8,128)(2,1)S(1)}, bf16[6,32,512]{2,1,0:T(8,128)(2,1)S(1)}, u32[]{:S(2)}, u32[]{:S(2)}) collective-permute-start(bf16[6,32,512]{2,1,0:T(8,128)(2,1)S(1)} %get-tuple-element.52), channel_id=1, source_target_pairs={{0,96},{8,104},{16,112},{24,120},{32,0},{40,8},{48,16},{56,24},{64... | collective-permute-start | bytes 589832 | tf_op jit(solution)/shard_map/ppermute | solution.py:30
  139.5 7.8 %collective-permute-start.16 = (bf16[6,32,512]{2,1,0:T(8,128)(2,1)S(1)}, bf16[6,32,512]{2,1,0:T(8,128)(2,1)S(1)}, u32[]{:S(2)}, u32[]{:S(2)}) collective-permute-start(bf16[6,32,512]{2,1,0:T(8,128)(2,1)S(1)} %get-tuple-element.92), channel_id=1, source_target_pairs={{0,16},{8,24},{16,0},{24,8},{32,48},{40,56},{48,32},{56,40},{64,80... | collective-permute-start | bytes 589832 | tf_op jit(solution)/shard_map/ppermute | solution.py:30
  141.3 7.2 %collective-permute-start.17 = (bf16[6,32,512]{2,1,0:T(8,128)(2,1)S(1)}, bf16[6,32,512]{2,1,0:T(8,128)(2,1)S(1)}, u32[]{:S(2)}, u32[]{:S(2)}) collective-permute-start(bf16[6,32,512]{2,1,0:T(8,128)(2,1)S(1)} %get-tuple-element.52), channel_id=1, source_target_pairs={{0,64},{8,72},{16,80},{24,88},{32,96},{40,104},{48,112},{56,120},{... | collective-permute-start | bytes 589832 | tf_op jit(solution)/shard_map/ppermute | solution.py:30
  148.5 18.3 %collective-permute-start.22 = (bf16[4,6,32,512]{3,2,1,0:T(8,128)(2,1)S(1)}, bf16[4,6,32,512]{3,2,1,0:T(8,128)(2,1)S(1)}, u32[]{:S(2)}, u32[]{:S(2)}) collective-permute-start(bf16[4,6,32,512]{3,2,1,0:T(8,128)(2,1)S(1)} %pad_maximum_fusion.2.refs_1_), channel_id=1, source_target_pairs={{0,8},{8,16},{16,24},{24,0},{32,40},{40,48},{48,56},{56,32},{64,72... | collective-permute-start | bytes 2359304 | tf_op jit(solution)/shard_map/ppermute | solution.py:30
  149.6 17.6 %collective-permute-start.24 = (bf16[4,6,32,512]{3,2,1,0:T(8,128)(2,1)S(1)}, bf16[4,6,32,512]{3,2,1,0:T(8,128)(2,1)S(1)}, u32[]{:S(2)}, u32[]{:S(2)}) collective-permute-start(bf16[4,6,32,512]{3,2,1,0:T(8,128)(2,1)S(1)} %pad_maximum_fusion.2.refs_1_), channel_id=1, source_target_pairs={{0,24},{8,0},{16,8},{24,16},{32,56},{40,32},{48,40},{56,48},{64,88... | collective-permute-start | bytes 2359304 | tf_op jit(solution)/shard_map/ppermute | solution.py:30
  152.0 19.2 %collective-permute-start.18 = (bf16[4,6,32,512]{3,2,1,0:T(8,128)(2,1)S(1)}, bf16[4,6,32,512]{3,2,1,0:T(8,128)(2,1)S(1)}, u32[]{:S(2)}, u32[]{:S(2)}) collective-permute-start(bf16[4,6,32,512]{3,2,1,0:T(8,128)(2,1)S(1)} %pad_maximum_fusion.1.refs_0_), channel_id=1, source_target_pairs={{0,32},{8,40},{16,48},{24,56},{32,64},{40,72},{48,80},{56,88},{64,... | collective-permute-start | bytes 2359304 | tf_op jit(solution)/shard_map/ppermute | solution.py:30
  153.6 20.8 %collective-permute-start.20 = (bf16[4,6,32,512]{3,2,1,0:T(8,128)(2,1)S(1)}, bf16[4,6,32,512]{3,2,1,0:T(8,128)(2,1)S(1)}, u32[]{:S(2)}, u32[]{:S(2)}) collective-permute-start(bf16[4,6,32,512]{3,2,1,0:T(8,128)(2,1)S(1)} %pad_maximum_fusion.1.refs_0_), channel_id=1, source_target_pairs={{0,96},{8,104},{16,112},{24,120},{32,0},{40,8},{48,16},{56,24},{64... | collective-permute-start | bytes 2359304 | tf_op jit(solution)/shard_map/ppermute | solution.py:30
  166.9 19.2 %collective-permute-start.23 = (bf16[2,6,32,512]{3,2,1,0:T(8,128)(2,1)S(1)}, bf16[2,6,32,512]{3,2,1,0:T(8,128)(2,1)S(1)}, u32[]{:S(2)}, u32[]{:S(2)}) collective-permute-start(bf16[2,6,32,512]{3,2,1,0:T(8,128)(2,1)S(1)} %slice.41), channel_id=1, source_target_pairs={{0,8},{8,16},{16,24},{24,0},{32,40},{40,48},{48,56},{56,32},{64,72... | collective-permute-start | bytes 1179656 | tf_op jit(solution)/shard_map/ppermute | solution.py:30
  168.0 18.1 %collective-permute-start.25 = (bf16[2,6,32,512]{3,2,1,0:T(8,128)(2,1)}, bf16[2,6,32,512]{3,2,1,0:T(8,128)(2,1)S(1)}, u32[]{:S(2)}, u32[]{:S(2)}) collective-permute-start(bf16[2,6,32,512]{3,2,1,0:T(8,128)(2,1)} %slice.42), channel_id=1, source_target_pairs={{0,24},{8,0},{16,8},{24,16},{32,56},{40,32},{48,40},{56,48},{64,88... | collective-permute-start | bytes 1179656 | tf_op jit(solution)/shard_map/ppermute | solution.py:30
  172.0 14.1 %collective-permute-start.19 = (bf16[2,6,32,512]{3,2,1,0:T(8,128)(2,1)}, bf16[2,6,32,512]{3,2,1,0:T(8,128)(2,1)S(1)}, u32[]{:S(2)}, u32[]{:S(2)}) collective-permute-start(bf16[2,6,32,512]{3,2,1,0:T(8,128)(2,1)} %slice.39), channel_id=1, source_target_pairs={{0,32},{8,40},{16,48},{24,56},{32,64},{40,72},{48,80},{56,88},{64,... | collective-permute-start | bytes 1179656 | tf_op jit(solution)/shard_map/ppermute | solution.py:30
  175.2 10.9 %collective-permute-start.21 = (bf16[2,6,32,512]{3,2,1,0:T(8,128)(2,1)}, bf16[2,6,32,512]{3,2,1,0:T(8,128)(2,1)S(1)}, u32[]{:S(2)}, u32[]{:S(2)}) collective-permute-start(bf16[2,6,32,512]{3,2,1,0:T(8,128)(2,1)} %slice.40), channel_id=1, source_target_pairs={{0,96},{8,104},{16,112},{24,120},{32,0},{40,8},{48,16},{56,24},{64... | collective-permute-start | bytes 1179656 | tf_op jit(solution)/shard_map/ppermute | solution.py:30
Sparse Core Ops, SparseCore 0:
  9.7 63.3 all-gather.7
  85.8 28.2 all-gather.5
  130.6 27.1 all-gather.9
